TPU v7x, 32 devices: a whole 2x2x4 slice. The times are simulated.
32 devices in a mesh: dp: 2 (over x), row: 4 (over y, core), col: 4 (over z).
Axes of the slice: x: 2, y: 2, z: 4, core: 2. Of those that a mesh axis runs over, the one named last changes fastest.
Arguments:
- tokens: bfloat16 [4096, 1600], P(('dp', 'row'), 'col'), may hold values from -6 to 6
- cotangent: bfloat16 [4096, 1600], P(('dp', 'row'), 'col'), may hold values from -6 to 6
- segments: int32 [4096], P('dp'), may hold values from 0 to 23, as said below
- w_heads: float32 [4, 2, 200, 3, 1600], P('col', 'dp', None, None, 'row'), may hold values from -0.15625 to 0.15625
- w_out: float32 [4, 2, 200, 1600], P('row', 'dp', None, 'col'), may hold values from -0.875 to 0.875
- w_up: float32 [4, 2, 200, 4, 1600], P('col', 'dp', None, None, 'row'), may hold values from -0.15625 to 0.15625
- w_down: float32 [4, 4, 2, 200, 1600], P(None, 'row', 'dp', None, 'col'), may hold values from -0.078125 to 0.078125
- norm_vectors: float32 [2, 4, 2, 200], P(None, 'col', 'dp'), as said below
- width_vectors: float32 [4, 4, 2, 200], P(None, 'col', 'dp'), as said below
- attend_bias: float32 [2, 4, 2, 200], P(None, 'row', 'dp'), may hold values from -1.25 to 1.25
- hidden_vectors: float32 [4, 4, 2, 200], P(None, 'row', 'dp'), may hold values from -1.25 to 1.25
- drift_heads: float32 [4, 2, 200, 3, 1600], P('col', 'dp', None, None, 'row'), may hold values from -128 to 128
- drift_out: float32 [4, 2, 200, 1600], P('row', 'dp', None, 'col'), may hold values from -7 to 7
- drift_up: float32 [4, 2, 200, 4, 1600], P('col', 'dp', None, None, 'row'), may hold values from -12 to 12
- drift_down: float32 [4, 4, 2, 200, 1600], P(None, 'row', 'dp', None, 'col'), may hold values from -28 to 28
- drift_norm: float32 [2, 4, 2, 200], P(None, 'col', 'dp'), may hold values from -256 to 256
- drift_width: float32 [4, 4, 2, 200], P(None, 'col', 'dp')
- drift_attend: float32 [2, 4, 2, 200], P(None, 'row', 'dp'), may hold values from -128 to 128
- drift_hidden: float32 [4, 4, 2, 200], P(None, 'row', 'dp'), may hold values from -12 to 12
- power_heads: float32 [4, 2, 200, 3, 1600], P('col', 'dp', None, None, 'row'), may hold values from 47.18592 to 188.74368
- power_out: float32 [4, 2, 200, 1600], P('row', 'dp', None, 'col'), may hold values from 0.1152 to 0.4608
- power_up: float32 [4, 2, 200, 4, 1600], P('col', 'dp', None, None, 'row'), may hold values from 0.36864 to 1.47456
- power_down: float32 [4, 4, 2, 200, 1600], P(None, 'row', 'dp', None, 'col'), may hold values from 1.72032 to 6.88128
- power_norm: float32 [2, 4, 2, 200], P(None, 'col', 'dp'), may hold values from 131.072 to 524.288
- power_width: float32 [4, 4, 2, 200], P(None, 'col', 'dp'), as said below
- power_attend: float32 [2, 4, 2, 200], P(None, 'row', 'dp'), may hold values from 47.18592 to 188.74368
- power_hidden: float32 [4, 4, 2, 200], P(None, 'row', 'dp'), may hold values from 0.36864 to 1.47456
Outputs:
- result_tokens: bfloat16 [4096, 1600], P(('dp', 'row'), 'col')
- input_gradient: float32 [4096, 1600], P(('dp', 'row'), 'col')
- heads_drift: float32 [4, 2, 200, 3, 1600], P('col', 'dp', None, None, 'row')
- heads_power: float32 [4, 2, 200, 3, 1600], P('col', 'dp', None, None, 'row')
- heads_new: float32 [4, 2, 200, 3, 1600], P('col', 'dp', None, None, 'row')
- out_drift: float32 [4, 2, 200, 1600], P('row', 'dp', None, 'col')
- out_power: float32 [4, 2, 200, 1600], P('row', 'dp', None, 'col')
- out_new: float32 [4, 2, 200, 1600], P('row', 'dp', None, 'col')
- up_drift: float32 [4, 2, 200, 4, 1600], P('col', 'dp', None, None, 'row')
- up_power: float32 [4, 2, 200, 4, 1600], P('col', 'dp', None, None, 'row')
- up_new: float32 [4, 2, 200, 4, 1600], P('col', 'dp', None, None, 'row')
- down_drift: float32 [4, 4, 2, 200, 1600], P(None, 'row', 'dp', None, 'col')
- down_power: float32 [4, 4, 2, 200, 1600], P(None, 'row', 'dp', None, 'col')
- down_new: float32 [4, 4, 2, 200, 1600], P(None, 'row', 'dp', None, 'col')
- norm_drift: float32 [2, 4, 2, 200], P(None, 'col', 'dp')
- norm_power: float32 [2, 4, 2, 200], P(None, 'col', 'dp')
- norm_new: float32 [2, 4, 2, 200], P(None, 'col', 'dp')
- width_drift: float32 [4, 4, 2, 200], P(None, 'col', 'dp')
- width_power: float32 [4, 4, 2, 200], P(None, 'col', 'dp')
- width_new: float32 [4, 4, 2, 200], P(None, 'col', 'dp')
- attend_drift: float32 [2, 4, 2, 200], P(None, 'row', 'dp')
- attend_power: float32 [2, 4, 2, 200], P(None, 'row', 'dp')
- attend_new: float32 [2, 4, 2, 200], P(None, 'row', 'dp')
- hidden_drift: float32 [4, 4, 2, 200], P(None, 'row', 'dp')
- hidden_power: float32 [4, 4, 2, 200], P(None, 'row', 'dp')
- hidden_new: float32 [4, 4, 2, 200], P(None, 'row', 'dp')
Inputs may be any that keep to these rules, and one draw needn't show every extreme that they name: `segments`: never fall along the tokens; each sequence of 512 tokens holds three documents numbered for it alone, the second beginning within its first 128 tokens and the third within its last 128. `norm_vectors`: a gain about one in row 0, a shift in row 1. `width_vectors`: a gain about one in row 1, a shift and biases in the others. `power_width`: positive.
All inputs are finite; a program needn't handle non-finite values.
Results may differ from a plain program's by a relative error of at most 0.012.
Values may be sent and summed in bfloat16 or wider, within the bound.
A program may use at most 896 MiB of HBM per device.

v0:
```python
import functools

import jax
import jax.numpy as jnp
from jax import lax
from jax.experimental import pallas as pl
from jax.experimental.pallas import tpu as pltpu
from jax.sharding import PartitionSpec as P

HEADS = 25
HD = 64
TOK_DEV = 128
STEP = 10


NORM_EPSILON = 1e-05
BETA_FIRST = 0.9
BETA_SECOND = 0.999
ADAM_EPSILON = 1e-08
MATRIX_DECAY = 0.1
MASKED = -1e30
ROOT = (2.0 / 3.141592653589793) ** 0.5
CUBIC = 0.044715
VMEM_BYTES = 66 * 1024 * 1024


def adam(weight, gradient, first, second, rate, decay):
    first_new = BETA_FIRST * first + (1.0 - BETA_FIRST) * gradient
    second_new = BETA_SECOND * second + (1.0 - BETA_SECOND) * gradient * gradient
    corrected = first_new / (1.0 - BETA_FIRST**STEP)
    divisor = jnp.sqrt(second_new / (1.0 - BETA_SECOND**STEP)) + ADAM_EPSILON
    return (first_new, second_new, weight - rate * (corrected / divisor + decay * weight))


def smooth(values):
    return jax.nn.gelu(values, approximate=True)


def ceil_to(count, unit):
    return -(-count // unit) * unit


class Sizes:
    def __init__(self, share, pieces, seq):
        self.share = share
        self.pieces = pieces
        self.block = ceil_to(pieces, 16)
        self.pair = 2 * self.block
        self.width = 4 * self.pair
        self.seq = seq
        self.part = seq // 4
        self.both = 2 * seq
        self.main = (HEADS // 4) * HD
        self.slack = share - self.main
        self.heads = ceil_to(3 * share, 256)
        self.mixed = ceil_to(pieces + 1, 128)
        self.hidden = ceil_to(4 * pieces + 1, 128)
        self.tiles = self.width // 128
        self.solid = self.hidden - 128
        self.tail = 4 * pieces - self.solid
        assert 0 < self.tail < 64


class Place:
    def __init__(self):
        self.d, self.r, self.c = (lax.axis_index(name) for name in ("dp", "row", "col"))
        self.y, self.k = self.r // 2, self.r % 2

    def plane(self, mask):
        d = 1 - self.d if mask & 4 else self.d
        y = 1 - self.y if mask & 2 else self.y
        k = 1 - self.k if mask & 1 else self.k
        return d, 2 * y + k

    def peer(self, mask):
        d, r = self.plane(mask)
        return (d, r, self.c)

    def along(self, c):
        return (self.d, self.r, c)


def run(when, action):
    if when is None:
        action()
    else:
        pl.when(when)(action)


class Wires:
    def __init__(self, sends, arrivals):
        self.sends, self.arrivals = sends, arrivals
        self.used = 0
        self.open = []

    def make(self, source, target, index, slot, device):
        return pltpu.make_async_remote_copy(
            src_ref=source,
            dst_ref=target,
            send_sem=self.sends.at[index],
            recv_sem=self.arrivals.at[slot],
            device_id=device,
            device_id_type=pl.DeviceIdType.MESH,
        )

    def copy(self, source, target, device, slot, when=None):
        made = self.make(source, target, self.used, slot, device)
        self.used += 1
        run(when, made.start)
        item = (when, made)
        self.open.append(item)
        return item

    def arrived(self, target, slot, device, when=None):
        run(when, self.make(target, target, 0, slot, device).wait_recv)

    def close(self, some=None):
        for item in self.open if some is None else some:
            run(item[0], item[1].wait_send)
        self.open = [] if some is None else [o for o in self.open if all(o is not s for s in some)]


def greet(at, diagonal):
    barrier = pltpu.get_barrier_semaphore()

    def signal(device):
        pl.semaphore_signal(
            barrier, inc=1, device_id=device, device_id_type=pl.DeviceIdType.MESH
        )

    for mask in range(1, 8):
        signal(at.peer(mask))
    for c in range(4):
        run(at.c != c, functools.partial(signal, (at.d, at.r, c)))
        if diagonal:
            run(at.c != c, functools.partial(signal, (1 - at.d, at.r, c)))
    run(at.r != at.c, functools.partial(signal, (at.d, at.c, at.r)))
    pl.semaphore_wait(barrier, (13 if diagonal else 10) + jnp.where(at.r != at.c, 1, 0))


def rows_at(start, size):
    return pl.ds(pl.multiple_of(start, 16), size)


def lanes_at(start, size):
    return pl.ds(pl.multiple_of(start, 128), size)


def choose(shape, source):
    rows = lax.broadcasted_iota(jnp.int32, shape, 0)
    wanted = source(lax.broadcasted_iota(jnp.int32, shape, 1))
    return (rows == wanted).astype(jnp.bfloat16)


def edge_source(column):
    part, place = column // HD, column % HD
    wanted = jnp.where(place >= 16, 128 * part + place - 16, 384 + 16 * part + place)
    return jnp.where(part < 3, wanted, -1)


def spread_source(column):
    part, place = column // 128, column % 128
    return jnp.where(place < HD, HD * part + place, -1)


def picked(values, table):
    return jnp.dot(values, table, preferred_element_type=jnp.float32).astype(jnp.bfloat16)


def times(left, right):
    return jnp.dot(left, right, preferred_element_type=jnp.float32)


def times_flipped(left, right):
    return lax.dot_general(
        left, right, (((1,), (1,)), ((), ())), preferred_element_type=jnp.float32
    )


def times_outer(left, right):
    return lax.dot_general(
        left, right, (((0,), (0,)), ((), ())), preferred_element_type=jnp.float32
    )


def over_tiles(total, action, tile=256):
    @pl.loop(0, total // tile)
    def _(i):
        action(i * tile, tile)

    if total % tile:
        action(total - total % tile, total % tile)


def turned(values):
    return values.astype(jnp.float32).T


def gather_group(wires, masks, region, at, base):
    own = region(*at.plane(0))
    sent = [wires.copy(own, own, at.peer(mask), base + mask) for mask in (1, *masks)]

    def finish():
        for mask in masks:
            there = region(*at.plane(mask))
            wires.arrived(there, base + mask, at.peer(mask))
            sent.append(wires.copy(there, there, at.peer(1), base + mask + 1))
        for mask in (0, *masks):
            there = region(*at.plane(mask | 1))
            wires.arrived(there, base + (mask | 1), at.peer(1))

    return finish, sent


def cross_over(wires, home, landing, region, at, base):
    rows = home.shape[0] // 2
    wires.copy(home.at[rows_at(rows * (1 - at.y), rows)], landing, at.peer(2), base)
    target = region(at.c, at.d, at.y)

    def along(source, s):
        wires.copy(source, target, at.along(s), base + 1 + at.c, s != at.c)

        @pl.when(s == at.c)
        def _():
            target[...] = source[...]

    along(home.at[rows_at(rows * at.y, rows)], at.r)

    def onward():
        wires.arrived(landing, base, at.peer(2))
        along(landing, 2 * (1 - at.y) + at.k)

    def finish():
        for c in range(4):
            needed = (at.k == at.c % 2) & (at.c != c)
            wires.arrived(region(c, at.d, at.y), base + 1 + c, at.along(c), needed)

    return onward, finish


def share_pieces(wires, masks, region, at, base):
    holds = at.k == at.c % 2
    near = base + 4 * len(masks)

    def place(mask):
        d, r = at.plane(mask)
        return d, r // 2

    for c in range(4):
        own = region(c, *place(0))
        for i, mask in enumerate(masks):
            wires.copy(own, own, at.peer(mask), base + 4 * i + c, holds)
    for c in range(4):
        own = region(c, *place(0))
        wires.copy(own, own, at.peer(1), near + c, holds)

    def finish():
        for i, mask in enumerate(masks):
            for c in range(4):
                there = region(c, *place(mask))
                wires.arrived(there, base + 4 * i + c, at.peer(mask), holds)
                wires.copy(there, there, at.peer(1), near + 4 * (i + 1) + c, holds)
        for i, mask in enumerate((0, *masks)):
            for c in range(4):
                there = region(c, *place(mask))
                wires.arrived(there, near + 4 * i + c, at.peer(1), jnp.logical_not(holds))

    return finish


def scatter_group(wires, masks, partial, chunk, near, mid, far, at, base):
    sent = []
    for i, mask in enumerate((0, *masks)):
        rows = rows_at(chunk(*at.plane(mask | 1)), near.shape[1])
        sent.append(wires.copy(partial.at[rows], near.at[i], at.peer(1), base + i))

    def rows_of(mask):
        return rows_at(chunk(*at.plane(mask)), near.shape[1])

    def onward():
        for i, mask in enumerate((0, *masks)):
            wires.arrived(near.at[i], base + i, at.peer(1))
        for i, mask in enumerate(masks):
            both = partial[rows_of(mask)].astype(jnp.float32) + near[i + 1].astype(jnp.float32)
            mid[i] = both.astype(jnp.bfloat16)
            sent.append(wires.copy(mid.at[i], far.at[i], at.peer(mask), base + 4 + i))

    def total():
        for i, mask in enumerate(masks):
            wires.arrived(far.at[i], base + 4 + i, at.peer(mask))
        result = partial[rows_of(0)].astype(jnp.float32) + near[0].astype(jnp.float32)
        for i in range(len(masks)):
            result = result + far[i].astype(jnp.float32)
        return result

    return onward, total, sent


def spread_col(wires, region, at, base, wait=False):
    own = region(at.c)

    def send(distance):
        for delta in (distance, -distance):
            there = at.c + delta
            wires.copy(own, own, at.along(there), base + at.c, (there >= 0) & (there < 4))

    if not wait:
        send(2)
        send(1)

    def relay():
        for here, start, end in ((2, 0, 3), (1, 3, 0)):
            block = region(start)
            wires.arrived(block, base + start, at.along(start), at.c == here)
            wires.copy(block, block, at.along(end), base + start, at.c == here)

    def finish():
        for c in range(4):
            needed = at.c != c
            if c == 0:
                needed = needed & (at.c != 2)
            if c == 3:
                needed = needed & (at.c != 1)
            wires.arrived(region(c), base + c, at.along(c), needed)

    return (send, relay, finish) if wait else (relay, finish)


def collect_col(wires, piece, landing, rest, at, base, direct=None):
    low_end, high_end = at.c == 0, at.c == 3
    ends = low_end | high_end
    via = jnp.where(low_end, 1, 2)

    def pick(*choices):
        return jnp.where(
            low_end,
            choices[0],
            jnp.where(at.c == 1, choices[1], jnp.where(high_end, choices[3], choices[2])),
        )

    order = (pick(3, 0, 3, 0), pick(2, 2, 1, 1), pick(1, 3, 0, 2), at.c)
    target = landing.at[at.c]

    def send(step):
        there = order[step]
        block = (direct or piece)(there)
        if step == 0:
            wires.copy(block, rest, at.along(via), base + 4, ends)
            wires.copy(block, target, at.along(there), base + at.c, jnp.logical_not(ends))
        elif step == 1:
            wires.copy(block, target, at.along(there), base + at.c)
        elif step == 2:
            wires.copy(block, target, at.along(there), base + at.c, ends)

    def relay(add):
        @pl.when(jnp.logical_not(ends))
        def _():
            wires.make(rest, rest, 0, base + 4, at.along(0)).wait_recv()
            add(order[2])

        wires.copy(piece(order[2]), target, at.along(order[2]), base + at.c, jnp.logical_not(ends))

    def arrived(c):
        wires.arrived(landing.at[c], base + c, at.along(c), sent_from(c))

    def sent_from(c):
        here = at.c != c
        if c in (0, 3):
            here = here & (at.c != 3 - c)
        return here

    return order, send, relay, arrived, sent_from


def forward_kernel(
    sz,
    x_home_in,
    dy_home_in,
    w_heads,
    w_out,
    w_up,
    w_down,
    norm_vectors,
    width_vectors,
    attend_bias,
    hidden_vectors,
    segments,
    wh_out,
    wo_out,
    wu_out,
    wd_out,
    h1_t_out,
    h2_t_out,
    gd_out,
    gt_out,
    dy_out,
    u_out,
    gl_out,
    qw_out,
    kw_out,
    vw_out,
    a_nat_out,
    lse_out,
    x2_out,
    x_own_out,
    vec_rows_out,
    wh,
    wo,
    wu,
    wd,
    h1_t,
    h2_t,
    gd,
    gt,
    dy_t,
    dy,
    u,
    gl,
    qw,
    kw,
    vw,
    a_nat,
    lse,
    x2,
    x_own,
    vec_rows,
    x_t,
    h1,
    h2,
    own_qkv,
    aw,
    vec,
    part,
    edge_out,
    edge_in,
    edge_back,
    near,
    mid,
    far,
    x_raw,
    dy_raw,
    heads_raw,
    out_raw,
    up_raw,
    down_raw,
    x_home,
    dy_home,
    wu_own,
    wd_tail,
    col_labels,
    x_half,
    dy_half,
    sends,
    arrivals,
    locals_,
):
    at = Place()
    wires = Wires(sends, arrivals)
    low = jnp.bfloat16
    pair, block, pieces = sz.pair, sz.block, sz.pieces
    fetched = []
    for i, (source, target) in enumerate(
        (
            (x_home_in, x_raw),
            (w_heads, heads_raw),
            (w_up, up_raw),
            (w_out, out_raw),
            (w_down, down_raw),
            (dy_home_in, dy_raw),
        )
    ):
        fetched.append(pltpu.make_async_copy(source, target, locals_.at[40 + i]))
        fetched[i].start()
    row_labels = segments.at[:, lanes_at(sz.seq * at.c, sz.seq)]

    def halves(value, target):
        value = value.astype(jnp.float32)
        gap = jnp.zeros((block - pieces, value.shape[1]), jnp.float32)
        parts = [value[0:pieces], gap, value[pieces : 2 * pieces], gap]
        target[...] = jnp.concatenate(parts, axis=0).astype(low)

    def quarter(row):
        return row.astype(low).astype(jnp.float32) * 0.25

    def placed(row):
        both = jnp.concatenate([row, row], axis=1)
        half_of = lax.broadcasted_iota(jnp.int32, both.shape, 1) // pieces
        return jnp.where(half_of == at.d, both, 0.0)

    def with_row(value, row):
        gap = jnp.zeros((block - pieces - 1, value.shape[1]), jnp.float32)
        return jnp.concatenate([value, row, gap], axis=0)

    flat = jnp.concatenate(
        [norm_vectors[0], norm_vectors[1], width_vectors[1], width_vectors[2]], axis=0
    )
    flat = jnp.concatenate([flat, jnp.zeros((124, pieces), jnp.float32)], axis=0)
    flat = jnp.concatenate([flat, jnp.zeros((128, 256 - pieces), jnp.float32)], axis=1)
    where_row = lax.broadcasted_iota(jnp.int32, flat.shape, 0)
    where_lane = lax.broadcasted_iota(jnp.int32, flat.shape, 1)
    carrier = (where_lane == pieces) & ((where_row == 1) | (where_row == 3))
    own_rows = rows_at(pair * at.c + block * at.d, block)
    vec[own_rows] = jnp.where(carrier, 1.0, flat).T[0:block].astype(low)
    fetched[0].wait()
    halves(x_raw[...], x_home)
    greet(at, False)

    def x_piece(c, d, y):
        return x_t.at[rows_at(pair * c + block * y, block)]

    def dy_piece(c, d, y):
        return dy_t.at[rows_at(pair * c + block * y, block), lanes_at(sz.seq * d, sz.seq)]

    used = [0]

    def flush(source, target):
        made = pltpu.make_async_copy(source, target, locals_.at[used[0]])
        used[0] += 1
        made.start()
        flushed.append(made)

    flushed = []

    def vec_block(d, c):
        return vec.at[rows_at(pair * c + block * d, block)]

    def wh_block(d):
        return lambda c: wh.at[rows_at(pair * c + block * d, block)]

    def wo_block(d):
        return lambda c: wo.at[rows_at(pair * c, pair), lanes_at(sz.mixed * d, sz.mixed)]

    def wu_block(d):
        return lambda c: wu.at[rows_at(pair * c + block * d, block)]

    def wd_block(half):
        return lambda c: wd.at[rows_at(pair * c + block * half, block)]

    x_onward, x_crossed = cross_over(wires, x_home, x_half, x_piece, at, 96)
    for c in range(4):
        wires.copy(vec_block(at.d, at.c), vec_block(at.d, at.c), at.along(c), 2 + at.c, at.c != c)
    wires.copy(vec_block(at.d, at.c), vec_block(at.d, at.c), at.peer(4), 6 + at.c)

    fetched[1].wait()
    for r in range(4):

        @pl.when(at.r == r)
        def _():
            cut = sz.share - sz.slack * r
            tails = []
            for i in range(3):
                value = heads_raw[i]
                row = jnp.zeros((1, sz.share), jnp.float32)
                if i != 1:
                    row = placed(quarter(attend_bias[i // 2]))
                value = with_row(value, row)
                if r:
                    value = jnp.concatenate([value[:, cut:], value[:, 0:cut]], axis=1)
                wh[own_rows, sz.main * i : sz.main * (i + 1)] = value[:, 0 : sz.main].astype(low)
                tails.append(value[:, sz.main :])
            tails.append(jnp.zeros((block, sz.heads - 3 * sz.share), jnp.float32))
            wh[own_rows, 3 * sz.main : sz.heads] = jnp.concatenate(tails, axis=1).astype(low)

    x_onward()
    wh_relay, wh_done = spread_col(wires, wh_block(at.d), at, 20)
    wires.copy(wh_block(at.d)(at.c), wh_block(at.d)(at.c), at.peer(4), 24 + at.c)

    fetched[2].wait()
    gap = jnp.zeros((block, sz.hidden - 4 * pieces), jnp.float32)
    values = [
        with_row(up_raw[:, j, :], placed(quarter(hidden_vectors[j]))) for j in range(4)
    ]
    for i in range(2):
        lanes = slice(pieces * i, pieces * (i + 1))
        whole = jnp.concatenate([value[:, lanes] for value in values] + [gap], axis=1)

        @pl.when(at.d == i)
        def _():
            wu[own_rows] = whole.astype(low)

        @pl.when(at.d != i)
        def _():
            wu_own[...] = whole.astype(low)

    wires.copy(wu_own, wu_block(at.d)(at.c), at.peer(4), 10)

    def turned_halves(value, target, rows, lanes):
        flipped = value.T
        gap = jnp.zeros((block - pieces, flipped.shape[1]), jnp.float32)
        parts = [flipped[0:pieces], gap, flipped[pieces : 2 * pieces], gap]
        target[rows, lanes] = jnp.concatenate(parts, axis=0).astype(low)

    fetched[3].wait()
    value = with_row(out_raw[...], placed(quarter(width_vectors[0])))
    value = jnp.concatenate([value, jnp.zeros((sz.mixed - block, sz.share), jnp.float32)], axis=0)
    for i in range(sz.mixed // 128):
        lanes = slice(128 * i, 128 * (i + 1))
        turned_halves(
            value[lanes], wo, rows_at(pair * at.c, pair), lanes_at(sz.mixed * at.d + 128 * i, 128)
        )
    wo_relay, wo_done = spread_col(wires, wo_block(at.d), at, 28)
    wires.copy(wo_block(at.d)(at.c), wo_block(at.d)(at.c), at.peer(4), 32 + at.c)

    fetched[5].wait()
    halves(dy_raw[...], dy_home)
    dy_onward, dy_crossed = cross_over(wires, dy_home, dy_half, dy_piece, at, 116)

    x_crossed()
    x_done = share_pieces(wires, (2,), x_piece, at, 104)

    fetched[4].wait()
    for i in range(sz.solid // 128):
        rows = slice(128 * i, 128 * (i + 1))
        turned_halves(down_raw[rows], wd, rows_at(pair * at.c, pair), rows)
    value = [
        jnp.zeros((64, sz.share), jnp.float32),
        down_raw[sz.solid : 4 * pieces],
        placed(quarter(width_vectors[3])),
        jnp.zeros((63 - sz.tail, sz.share), jnp.float32),
    ]
    turned_halves(jnp.concatenate(value, axis=0), wd_tail, slice(0, pair), slice(0, 128))

    def add_tail(d):
        rows = rows_at(pair * at.c + block * d, block)
        both = wu[rows, sz.solid : sz.hidden].astype(jnp.float32)
        both = both + wd_tail[rows_at(block * d, block)].astype(jnp.float32)
        wu[rows, sz.solid : sz.hidden] = both.astype(low)

    add_tail(at.d)
    col_labels[...] = jnp.concatenate([row_labels[...]] * 8, axis=0).astype(jnp.float32).T[:, 0:1]
    x_done()
    dy_onward()
    wires.arrived(wu_block(1 - at.d)(at.c), 10, at.peer(4))
    add_tail(1 - at.d)
    wu_first_send, wu_first, wu_first_done = spread_col(wires, wu_block(at.d), at, 36, True)
    wu_second_send, wu_second, wu_second_done = spread_col(wires, wu_block(1 - at.d), at, 40, True)
    for distance in (2, 1):
        wu_first_send(distance)
        wu_second_send(distance)

    for c in range(4):
        wires.arrived(vec_block(at.d, c), 2 + c, at.along(c), at.c != c)
    wires.arrived(vec_block(1 - at.d, at.c), 6 + at.c, at.peer(4))
    for step in range(1, 4):
        there = (at.c + step) % 4
        wires.copy(
            vec_block(at.d, there), vec_block(at.d, there), at.peer(4), 6 + there
        )
    for step in range(1, 4):
        there = (at.c + step) % 4
        wires.arrived(vec_block(1 - at.d, there), 6 + there, at.peer(4))
    features = 4.0 * sz.share

    def add_up(i, carry):
        rows = rows_at(128 * i, 128)
        value = x_t[rows].astype(jnp.float32)
        return (
            carry[0] + jnp.sum(value, axis=0, keepdims=True),
            carry[1] + jnp.sum(value * value, axis=0, keepdims=True),
        )

    zero = jnp.zeros((1, sz.seq), jnp.float32)
    sums = lax.fori_loop(0, sz.tiles, add_up, (zero, zero))
    center = sums[0] / features
    inverse = lax.rsqrt(sums[1] / features - center * center + NORM_EPSILON)

    @pl.loop(0, sz.tiles)
    def _(i):
        rows, lanes = rows_at(128 * i, 128), lanes_at(128 * i, 128)
        vectors = vec[rows].astype(jnp.float32)
        value = (x_t[rows].astype(jnp.float32) - center) * inverse
        value = value * vectors[:, 0:1] + vectors[:, 1:2]
        h1_t[rows] = value.astype(low)
        h1[:, lanes] = value.T.astype(low)
        mine = x_t[rows, lanes_at(sz.part * at.r, sz.part)]
        x_own[:, lanes] = turned(mine).astype(low)
        vec_rows[:, lanes] = vectors.T[0:8]

    flush(h1_t, h1_t_out)
    flush(x_own, x_own_out)
    flush(vec_rows, vec_rows_out)

    wh_relay()
    for c in range(4):
        needed = at.c != c
        if c == 0:
            needed = needed & (at.c != 2)
        if c == 3:
            needed = needed & (at.c != 1)
        wires.arrived(wh_block(at.d)(c), 20 + c, at.along(c), needed)
        wires.copy(wh_block(at.d)(c), wh_block(at.d)(c), at.peer(4), 24 + c, at.c != c)

    for c in range(4):
        wires.arrived(wh_block(1 - at.d)(c), 24 + c, at.peer(4))
    flush(wh, wh_out)

    @pl.loop(0, sz.heads // 256)
    def _(i):
        lanes = lanes_at(256 * i, 256)
        own_qkv[:, lanes] = times(h1[...], wh[:, lanes]).astype(low)

    starts = (0, sz.main, 2 * sz.main, 3 * sz.main)
    ends = jnp.concatenate([own_qkv[:, s : s + 128] for s in starts], axis=1)
    edge_out[...] = picked(ends, choose((512, 256), edge_source))
    last = at.r == 3

    @pl.when(at.r == 0)
    def _():
        edge_in[...] = jnp.zeros_like(edge_in)

    wires.copy(edge_out, edge_in, (at.d, at.r + 1, at.c), 52, at.r < 3)
    spread = choose((256, 384), spread_source)
    extra = picked(edge_out[...], spread)
    wires.arrived(edge_in, 52, (at.d, at.r - 1, at.c), at.r > 0)
    first = picked(edge_in[...], spread)
    lane = lax.broadcasted_iota(jnp.int32, (sz.seq, 128), 1)
    for i, target in enumerate((qw, kw, vw)):
        start = starts[i]
        target[:, 0:128] = jnp.where(
            lane < sz.slack * at.r,
            first[:, 128 * i : 128 * i + 128],
            own_qkv[:, start : start + 128],
        )
        target[:, 128 : sz.main] = own_qkv[:, start + 128 : start + sz.main]
        target[:, sz.main : sz.main + 128] = extra[:, 128 * i : 128 * i + 128]
    flush(qw, qw_out)
    flush(kw, kw_out)
    flush(vw, vw_out)

    wo_relay()
    for c in range(4):
        needed = at.c != c
        if c == 0:
            needed = needed & (at.c != 2)
        if c == 3:
            needed = needed & (at.c != 1)
        wires.arrived(wo_block(at.d)(c), 28 + c, at.along(c), needed)
        wires.copy(wo_block(at.d)(c), wo_block(at.d)(c), at.peer(4), 32 + c, at.c != c)

    dy_crossed()
    dy_done = share_pieces(wires, (2, 4, 6), dy_piece, at, 124)

    half = sz.seq // 2

    def heads_of(p, count):
        tile = lanes_at(128 * p, 128)
        for q in range(2):
            rows = slice(half * q, half * (q + 1))
            keys = half * (q + 1)
            order = lax.broadcasted_iota(jnp.int32, (half, keys), 0) + half * q
            allowed = (col_labels[rows, :] == row_labels[:, 0:keys].astype(jnp.float32)) & (
                order >= lax.broadcasted_iota(jnp.int32, (half, keys), 1)
            )
            lanes = lax.broadcasted_iota(jnp.int32, (half, 128), 1)
            side = lanes // HD
            total = jnp.zeros((half, 128), jnp.float32)
            for h in range(count):
                queries = jnp.where(side == h, qw[rows, tile].astype(jnp.float32) * HD ** (-0.5), 0.0)
                scores = times_flipped(queries.astype(low), kw[0:keys, tile])
                scores = jnp.where(allowed, scores, MASKED)
                highest = jnp.max(scores, axis=1, keepdims=True)
                raised = jnp.exp(scores - highest)
                summed = jnp.sum(raised, axis=1, keepdims=True)
                found = highest + jnp.log(summed)
                lse[rows, :] = jnp.where(lanes == 2 * p + h, found, lse[rows, :])
                soft = (raised * (1.0 / summed)).astype(low)
                total = jnp.where(side == h, times(soft, vw[0:keys, tile]), total)
            aw[rows, tile] = total.astype(low)

    lse[...] = jnp.zeros_like(lse)

    @pl.loop(0, sz.main // 128)
    def _(p):
        heads_of(p, 2)

    @pl.when(last)
    def _():
        heads_of(sz.main // 128, 1)
        edge_back[...] = aw[:, sz.main : sz.main + 128]

    flush(lse, lse_out)

    wires.copy(aw.at[:, 0:128], edge_back, (at.d, at.r - 1, at.c), 53, at.r > 0)
    wd_first_send, wd_first, wd_first_done = spread_col(wires, wd_block(0), at, 44, True)
    wd_second_send, wd_second, wd_second_done = spread_col(wires, wd_block(1), at, 48, True)
    for distance in (2, 1):
        wd_first_send(distance)
        wd_second_send(distance)
    wires.arrived(edge_back, 53, (at.d, at.r + 1, at.c), at.r < 3)

    def natural(column):
        inner = column % sz.mixed
        place = sz.pieces * (column // sz.mixed) + inner + sz.slack * at.r
        return jnp.where(inner < sz.pieces, place, -1)

    def natural_main(column):
        place = natural(column)
        return jnp.where(place < sz.main, place, -1)

    def natural_edge(column):
        return natural(column) - sz.main

    mixed = times(aw[:, 0 : sz.main], choose((sz.main, 2 * sz.mixed), natural_main))
    mixed = mixed + times(edge_back[...], choose((128, 2 * sz.mixed), natural_edge))
    ones = lax.broadcasted_iota(jnp.int32, mixed.shape, 1) % sz.mixed == sz.pieces
    a_nat[...] = jnp.where(ones, 1.0, mixed).astype(low)
    for c in range(4):
        wires.arrived(wo_block(1 - at.d)(c), 32 + c, at.peer(4))
    flush(wo, wo_out)
    flush(a_nat, a_nat_out)

    def project(start, tile):
        out = times_flipped(a_nat[...], wo[rows_at(start, tile)])
        part[:, lanes_at(start, tile)] = out.astype(low)

    over_tiles(sz.width, project)

    onward, total, _ = scatter_group(
        wires, (2,), part, lambda d, r: sz.part * r, near, mid, far, at, 64
    )
    onward()
    wu_first()
    wu_second()
    dy_done()
    middle = x_own[...].astype(jnp.float32) + total()
    x2[...] = middle
    flush(x2, x2_out)
    center = jnp.sum(middle, axis=1, keepdims=True) / features
    spread_two = jnp.sum(middle * middle, axis=1, keepdims=True) / features - center * center
    normed = (middle - center) * lax.rsqrt(spread_two + NORM_EPSILON)
    own_rows = rows_at(sz.part * (4 * at.d + at.r), sz.part)
    h2[own_rows] = (normed * vec_rows[2:3] + vec_rows[3:4]).astype(low)
    h2_done, _ = gather_group(
        wires, (2, 4, 6), lambda d, r: h2.at[rows_at(sz.part * (4 * d + r), sz.part)], at, 72
    )
    @pl.loop(0, sz.tiles)
    def _(i):
        dy[:, lanes_at(128 * i, 128)] = turned(dy_t[rows_at(128 * i, 128)]).astype(low)

    flush(dy, dy_out)
    h2_done()
    wu_first_done()
    wu_second_done()
    flush(wu, wu_out)

    def expand(start, tile):
        lanes = lanes_at(start, tile)
        value = times(h2[...], wu[:, lanes])
        u[:, lanes] = value
        inner = jnp.tanh(ROOT * (value + CUBIC * value * value * value))
        value = 0.5 * value * (1.0 + inner)
        if isinstance(start, int):
            column = lax.broadcasted_iota(jnp.int32, value.shape, 1)
            inside = (column >= 64) & (column < 64 + sz.tail)
            value = jnp.where(inside, pltpu.roll(value, 64, 1), 0.0)
            value = jnp.where(column == 64 + sz.tail, 1.0, value)
        gl[:, lanes] = value.astype(low)

    over_tiles(sz.hidden, expand)

    flush(u, u_out)
    flush(gl, gl_out)
    wd_first()

    @pl.loop(0, sz.tiles)
    def _(i):
        h2_t[rows_at(128 * i, 128)] = turned(h2[:, lanes_at(128 * i, 128)]).astype(low)

    flush(h2_t, h2_t_out)
    wd_second()

    @pl.loop(0, 4)
    def _(i):
        rows = rows_at(pair * i, pair)
        gd[rows] = times(dy_t[rows], gl[:, 0 : sz.solid]).astype(low)
        gt[rows] = times(dy_t[rows], gl[:, sz.solid : sz.hidden]).astype(low)

    flush(gd, gd_out)
    flush(gt, gt_out)
    wd_first_done()
    wd_second_done()
    flush(wd, wd_out)
    wires.close()
    for made in flushed:
        made.wait()


def backward_kernel(
    sz,
    dy_all,
    gd_all,
    gt_all,
    u_all,
    gl_all,
    h2_t_all,
    wd_all,
    wu_all,
    wo_all,
    wh_all,
    h1_t_all,
    qw_all,
    kw_all,
    vw_all,
    a_nat_all,
    lse_all,
    x2_all,
    x_own_all,
    vec_rows,
    segments,
    out_down,
    out_up,
    out_out,
    out_heads,
    result_home,
    grad_home,
    vec_out,
    zd,
    zu,
    zo,
    zh,
    res_all,
    res_two,
    grad_all,
    grad_two,
    rd,
    ru,
    ro,
    rh,
    qw,
    kw,
    vw,
    a_nat,
    lse,
    x2,
    x_own,
    xu,
    dy,
    dy_t,
    u,
    gl,
    h2_t,
    wd,
    wu,
    wo,
    wh,
    gt,
    dy_own,
    du,
    gw,
    gu,
    go,
    xh,
    xo,
    near_two,
    far_two,
    near_res,
    far_res,
    near_one,
    far_one,
    mid,
    dob,
    da,
    dk_sum,
    dv_sum,
    dx2,
    edge_out,
    edge_in,
    fore_out,
    fore_in,
    col_labels,
    res_stage,
    grad_stage,
    va,
    vb,
    sends,
    arrivals,
    locals_,
):
    at = Place()
    wires = Wires(sends, arrivals)
    low = jnp.bfloat16
    pair, block = sz.pair, sz.block
    features = 4.0 * sz.share
    used = [0]

    def load(source, target, when=None):
        made = pltpu.make_async_copy(source, target, locals_.at[used[0]])
        used[0] += 1
        run(when, made.start)
        return made

    own_rows = rows_at(sz.part * (4 * at.d + at.r), sz.part)
    gd = gw.at[:, 0 : sz.solid]
    loads = [
        load(s, t)
        for s, t in (
            (dy_all, dy),
            (wd_all, wd),
            (u_all, u),
            (dy_all.at[own_rows], dy_own),
            (wu_all, wu),
            (h2_t_all, h2_t),
            (gl_all, gl),
            (gd_all, gd),
            (wo_all, wo),
            (wh_all, wh),
            (x2_all, x2),
            (a_nat_all, a_nat),
            (qw_all, qw),
            (kw_all, kw),
            (vw_all, vw),
            (lse_all, lse),
            (x_own_all, x_own),
            (h1_t_all, dy_t.at[:, 0 : sz.seq]),
            (gt_all, gt),
        )
    ]
    greet(at, False)
    stay = []

    order, d_send, d_relay, d_arrived, d_from = collect_col(
        wires,
        lambda c: gd.at[rows_at(pair * c, pair)],
        zd,
        rd,
        at,
        0,
        lambda c: gd_all.at[rows_at(pair * c, pair)],
    )
    for step in range(4):
        d_send(step)

    def relay_of(rest, block):
        def add(there):
            rows = rows_at(pair * there, pair)
            block[rows] = (block[rows].astype(jnp.float32) + rest[...].astype(jnp.float32)).astype(low)

        return add

    for made in (*loads[0:3], loads[4]):
        made.wait()

    def through(start, tile):
        lanes = lanes_at(start, tile)
        last = isinstance(start, int)
        if last:
            upstream = pltpu.roll(times(dy[...], wu[:, lanes]), 64, 1)
        else:
            upstream = times(dy[...], wd[:, lanes])
        value = u[:, lanes]
        inner = jnp.tanh(ROOT * (value + CUBIC * value * value * value))
        slope = 0.5 * (1.0 + inner) + 0.5 * value * (1.0 - inner * inner) * ROOT * (
            1.0 + 3.0 * CUBIC * value * value
        )
        upstream = upstream * slope
        if last:
            column = lax.broadcasted_iota(jnp.int32, upstream.shape, 1)
            upstream = jnp.where(column < sz.tail, upstream, 0.0)
        du[:, lanes] = upstream.astype(low)

    over_tiles(sz.hidden, through)
    def back_up(start, tile):
        dy[:, lanes_at(start, tile)] = times_flipped(du[...], wu[rows_at(start, tile)]).astype(low)

    over_tiles(sz.width, back_up)

    def chunk_both(d, r):
        return sz.part * (4 * d + r)

    two_onward, two_total, two_sent = scatter_group(
        wires, (2, 4, 6), dy, chunk_both, near_two, mid, far_two, at, 16
    )
    loads[5].wait()
    loads[18].wait()
    order, u_send, u_relay, u_arrived, u_from = collect_col(
        wires, lambda c: gu.at[rows_at(pair * c, pair)], zu, ru, at, 5
    )
    for step in range(4):
        rows = rows_at(pair * order[step], pair)
        value = times(h2_t[rows], du[...])
        gu[rows, 0 : sz.solid] = value[:, 0 : sz.solid].astype(low)
        both = value[:, sz.solid : sz.hidden] + gt[rows].astype(jnp.float32)
        gu[rows, sz.solid : sz.hidden] = both.astype(low)
        u_send(step)
        if step == 1:
            two_onward()
    own = rows_at(pair * at.c, pair)
    gd_own = load(gd_all.at[own], h2_t.at[own, 0 : sz.solid])
    loads[7].wait()
    before = len(wires.open)
    d_relay(relay_of(rd, gd))
    gd_sends = wires.open[before:]

    def norm_back(upstream, values, gain):
        center = jnp.sum(values, axis=1, keepdims=True) / features
        spread = jnp.sum(values * values, axis=1, keepdims=True) / features - center * center
        inverse = lax.rsqrt(spread + NORM_EPSILON)
        centered = (values - center) * inverse
        scaled = upstream * gain
        inner = (
            scaled
            - jnp.sum(scaled, axis=1, keepdims=True) / features
            - centered * (jnp.sum(scaled * centered, axis=1, keepdims=True) / features)
        )
        return (
            inner * inverse,
            jnp.sum(upstream * centered, axis=0, keepdims=True),
            jnp.sum(upstream, axis=0, keepdims=True),
        )

    loads[10].wait()
    loads[3].wait()
    h2_back = two_total()
    through_norm, gain_two, shift_two = norm_back(h2_back, x2[...], vec_rows[2:3])
    middle_back = dy_own[...].astype(jnp.float32) + through_norm
    dx2[...] = middle_back
    va[0, 2:3] = gain_two
    va[0, 3:4] = shift_two
    va[0, 4:8] = jnp.zeros((4, sz.width), jnp.float32)
    dob[rows_at(sz.part * at.r, sz.part)] = middle_back.astype(low)
    dob_done, dob_sent = gather_group(
        wires, (2,), lambda d, r: dob.at[rows_at(sz.part * r, sz.part)], at, 24
    )

    def contract(start, tile):
        rows = rows_at(start, tile)
        out = times_flipped(gl[:, 0 : sz.solid], wd[rows])
        out = out + times_flipped(gl[:, sz.solid : sz.hidden], wu[rows, sz.solid : sz.hidden])
        dy[:, lanes_at(start, tile)] = out.astype(low)

    wires.close(two_sent)
    loads[6].wait()
    over_tiles(sz.width, contract)
    res_onward, res_total, res_sent = scatter_group(
        wires, (2, 4, 6), dy, chunk_both, near_res, mid, far_res, at, 32
    )

    dob_done()
    loads[11].wait()
    loads[8].wait()
    da[...] = times(dob[...], wo[...]).astype(low)
    slack, main = sz.slack, sz.main

    def from_natural(place):
        wanted = sz.mixed * (place // sz.pieces) + place % sz.pieces
        return jnp.where((place >= 0) & (place < sz.share), wanted, -1)

    fore_out[...] = picked(
        da[...], choose((2 * sz.mixed, 128), lambda j: from_natural(j + main - slack * at.r))
    )

    @pl.when(at.r == 0)
    def _():
        fore_in[...] = jnp.zeros_like(fore_in)

    wires.copy(fore_out, fore_in, (at.d, at.r + 1, at.c), 40, at.r < 3)

    @pl.loop(0, sz.tiles)
    def _(i):
        dy_t[rows_at(128 * i, 128), sz.seq : sz.both] = turned(dob[:, lanes_at(128 * i, 128)]).astype(low)

    res_onward()

    for step in range(4):
        there = (at.c + step) % 4
        rows = rows_at(pair * there, pair)
        go[rows] = times(dy_t[rows, sz.seq : sz.both], a_nat[...]).astype(low)
        wires.copy(
            go.at[rows, lanes_at(sz.mixed * (1 - at.d), sz.mixed)], xo.at[there], at.peer(4), 48 + there
        )
    wires.arrived(fore_in, 40, (at.d, at.r - 1, at.c), at.r > 0)
    window = times(da[...], choose((2 * sz.mixed, main), lambda j: from_natural(j - slack * at.r)))
    da_first = window[:, 0:128] + fore_in[...].astype(jnp.float32)
    da[:, 128:main] = window[:, 128:main].astype(low)
    da[:, 0:128] = da_first.astype(low)
    da[:, main : main + 128] = fore_out[...]

    row_labels = segments.at[:, lanes_at(sz.seq * at.c, sz.seq)]
    col_labels[...] = jnp.concatenate([row_labels[...]] * 8, axis=0).astype(jnp.float32).T[:, 0:1]
    for made in loads[12:17]:
        made.wait()
    half = sz.seq // 2
    dqw, dkw = (du.at[sz.seq * i : sz.seq * (i + 1), 0 : main + 128] for i in range(2))
    dvw = gl.at[0 : sz.seq, 0 : main + 128]

    def heads_back(p, count):
        tile = lanes_at(128 * p, 128)
        dk_sum[...] = jnp.zeros_like(dk_sum)
        dv_sum[...] = jnp.zeros_like(dv_sum)
        for q in range(2):
            rows = slice(half * q, half * (q + 1))
            keys = half * (q + 1)
            order = lax.broadcasted_iota(jnp.int32, (half, keys), 0) + half * q
            allowed = (col_labels[rows, :] == row_labels[:, 0:keys].astype(jnp.float32)) & (
                order >= lax.broadcasted_iota(jnp.int32, (half, keys), 1)
            )
            lanes = lax.broadcasted_iota(jnp.int32, (half, 128), 1)
            side = lanes // HD
            total = jnp.zeros((half, 128), jnp.float32)
            for h in range(count):
                queries = jnp.where(side == h, qw[rows, tile].astype(jnp.float32) * HD ** (-0.5), 0.0)
                queries = queries.astype(low)
                pulled = jnp.where(side == h, da[rows, tile].astype(jnp.float32), 0.0).astype(low)
                found = jnp.sum(jnp.where(lanes == 2 * p + h, lse[rows, :], 0.0), axis=1, keepdims=True)
                scores = times_flipped(queries, kw[0:keys, tile])
                soft = jnp.where(allowed, jnp.exp(jnp.where(allowed, scores - found, MASKED)), 0.0)
                soft_back = times_flipped(pulled, vw[0:keys, tile])
                inner = jnp.sum(soft_back * soft, axis=1, keepdims=True)
                score_back = (soft * (soft_back - inner)).astype(low)
                piece = times(score_back, kw[0:keys, tile]) * HD ** (-0.5)
                total = jnp.where(side == h, piece, total)
                dk_sum[0:keys] += times_outer(score_back, queries)
                dv_sum[0:keys] += times_outer(soft.astype(low), pulled)
            dqw[rows, tile] = total.astype(low)
        dkw[:, tile] = dk_sum[...].astype(low)
        dvw[:, tile] = dv_sum[...].astype(low)

    @pl.loop(0, main // 128)
    def _(p):
        heads_back(p, 2)

    @pl.when(at.r == 3)
    def _():
        heads_back(main // 128, 1)

    def compact(column):
        part, place = column // HD, column % HD
        return jnp.where(part < 3, 128 * part + place, -1)

    table = choose((384, 256), compact)
    backs = (dqw, dkw, dvw)
    edge_out[...] = picked(jnp.concatenate([b[:, 0:128] for b in backs], axis=1), table)
    wires.copy(edge_out, edge_in, (at.d, at.r - 1, at.c), 41, at.r > 0)

    @pl.when(at.r == 3)
    def _():
        edge_in[...] = picked(jnp.concatenate([b[:, main : main + 128] for b in backs], axis=1), table)

    u_relay(relay_of(ru, gu))

    def go_home(values, stage, every, halves, out, base):
        flipped = values.T
        for c in range(4):
            for y in range(2):
                rows = slice(pair * c + block * y, pair * c + block * (y + 1))
                stage[c, y] = flipped[rows].astype(low)
        holds = at.k == at.c % 2
        lanes = lanes_at(sz.part * at.r, sz.part)
        held = []
        for y in range(2):
            there = 2 * y + at.c % 2
            wires.copy(
                stage.at[:, y], every.at[:, :, lanes], (at.d, there, at.c), base + at.r, there != at.r
            )
            held.append((there == at.r, load(stage.at[:, y], every.at[:, :, lanes], there == at.r)))

        def along():
            for r in range(4):
                block_r = every.at[:, :, sz.part * r : sz.part * (r + 1)]
                wires.arrived(block_r, base + r, (at.d, r, at.c), holds & (at.r != r))
            for when, made in held:
                run(when, made.wait)
            del held[:]
            for c in range(4):
                wires.copy(
                    every.at[c], halves.at[at.c // 2], at.along(c), base + 4 + at.c // 2, holds & (at.c != c)
                )
                when = holds & (at.c == c)
                held.append((when, load(every.at[c], halves.at[at.c // 2], when)))

        def across():
            for when, made in held:
                run(when, made.wait)
            for t in range(2):
                there = 2 * t + at.k
                wires.arrived(halves.at[t], base + 4 + t, at.along(there), there != at.c)
            mine = out.at[rows_at(block * at.y, block)]
            wires.copy(halves.at[1 - at.y], mine, at.peer(2), base + 6)
            stay.append(load(halves.at[at.y], mine))

        def finish():
            wires.arrived(out.at[rows_at(block * (1 - at.y), block)], base + 6, at.peer(2))

        return along, across, finish

    res_along, res_across, res_finish = go_home(
        x2[...] + res_total(), res_stage, res_all, res_two, result_home, 56
    )
    wires.close(res_sent)

    wires.arrived(edge_in, 41, (at.d, at.r + 1, at.c), at.r < 3)

    def unfold(column):
        tile, lane = column // 128, column % 128
        inside = jnp.where(lane < HD - 16, HD * tile + lane + 16, -1)
        tail = jnp.where(lane < 48, HD * (lane // 16) + lane % 16, -1)
        return jnp.where(tile < 3, inside, tail)

    edges = picked(edge_in[...], choose((256, 512), unfold))
    lane = lax.broadcasted_iota(jnp.int32, (sz.seq, 128), 1)
    pieces = []
    for i, back in enumerate(backs):
        first = jnp.where(lane < slack * at.r, edges[:, 128 * i : 128 * i + 128], back[:, 0:128])
        pieces += [first, back[:, 128:main]]
    pieces.append(edges[:, 384:512])
    wires.close(dob_sent)
    own_back = dob.at[:, 0 : sz.heads]
    own_back[...] = jnp.concatenate(pieces, axis=1)

    wires.close(gd_sends)
    gd_own.wait()
    loads[17].wait()
    h_order, h_send, h_relay, h_arrived, h_from = collect_col(
        wires, lambda c: xh.at[c], zh, rh, at, 72
    )
    for step in range(4):
        there = h_order[step]
        rows = rows_at(pair * there, pair)
        gw[rows] = times(dy_t[rows, 0 : sz.seq], own_back[...]).astype(low)
        other = gw.at[rows_at(pair * there + block * (1 - at.d), block)]
        wires.copy(other, xh.at[there], at.peer(4), 80 + there)

    def o_heads(step):
        there = h_order[step]
        wires.arrived(xh.at[there], 80 + there, at.peer(4))
        mine = rows_at(pair * there + block * at.d, block)
        xh[there] = (gw[mine].astype(jnp.float32) + xh[there].astype(jnp.float32)).astype(low)
        h_send(step)

    for made in loads[9:10]:
        made.wait()

    def back_in(start, tile):
        out = times_flipped(own_back[...], wh[rows_at(start, tile)])
        dy[0 : sz.seq, lanes_at(start, tile)] = out.astype(low)

    over_tiles(sz.width, back_in)
    one_onward, one_total, _ = scatter_group(
        wires, (2,), dy, lambda d, r: sz.part * r, near_one, mid, far_one, at, 64
    )
    order, o_send, o_relay, o_arrived, o_from = collect_col(
        wires, lambda c: xo.at[c], zo, ro, at, 10
    )
    for step in range(4):
        there = order[step]
        wires.arrived(xo.at[there], 48 + there, at.peer(4))
        mine = go[rows_at(pair * there, pair), lanes_at(sz.mixed * at.d, sz.mixed)]
        xo[there] = (mine.astype(jnp.float32) + xo[there].astype(jnp.float32)).astype(low)
        o_send(step)

    def relay_out(there):
        both = xo[there].astype(jnp.float32) + ro[...].astype(jnp.float32)
        xo[there] = both.astype(low)

    brought = []

    def bring(c, landing, needed, lanes):
        made = load(landing.at[c], h2_t.at[pair * c : pair * (c + 1), 0:lanes], needed)
        brought.append((needed, made))

        @pl.when(jnp.logical_not(needed) & (at.c != c))
        def _():
            h2_t[pair * c : pair * (c + 1), 0:lanes] = jnp.zeros((pair, lanes), low)

    def summed(lanes):
        result = jnp.zeros((pair, lanes.stop - lanes.start), jnp.float32)
        for c in range(4):
            result = result + h2_t[pair * c : pair * (c + 1), lanes].astype(jnp.float32)
        return result

    half_rows = sz.pieces

    def natural_rows(value):
        flipped = value.T
        return jnp.concatenate(
            [flipped[:, 0:half_rows], flipped[:, block : block + half_rows]], axis=1
        )

    def own_half(row):
        return jnp.where(at.d == 0, row[:, 0:half_rows], row[:, half_rows : 2 * half_rows])

    def all_brought():
        for needed, made in brought:
            run(needed, made.wait)
        del brought[:]

    def relay_heads(there):
        xh[there] = (xh[there].astype(jnp.float32) + rh[...].astype(jnp.float32)).astype(low)

    res_along()
    one_onward()
    o_heads(0)
    h1_back = one_total()
    through_norm, gain_one, shift_one = norm_back(
        h1_back, x_own[...].astype(jnp.float32), vec_rows[0:1]
    )
    va[0, 0:1] = gain_one
    va[0, 1:2] = shift_one
    for mask in range(1, 8):
        wires.copy(va.at[0], va.at[mask], at.peer(mask), 84 + mask)
    grad_along, grad_across, grad_finish = go_home(
        dx2[...] + through_norm, grad_stage, grad_all, grad_two, grad_home, 104
    )
    for c in range(4):
        d_arrived(c)
        bring(c, zd, d_from(c), sz.solid)
    all_brought()
    for i in range(sz.solid // 128):
        rows = slice(128 * i, 128 * (i + 1))
        u[rows, 0 : sz.share] = natural_rows(summed(rows))
    down_out = load(u.at[0 : sz.solid, 0:512], out_down.at[0 : sz.solid])
    o_heads(1)
    grad_along()
    o_heads(2)
    h_relay(relay_heads)
    gu_own = load(gu.at[own], h2_t.at[own, 0 : sz.hidden])
    for c in range(4):
        u_arrived(c)
        bring(c, zu, u_from(c), sz.hidden)
    all_brought()
    gu_own.wait()
    value = natural_rows(summed(slice(sz.solid, sz.hidden)))
    end = 4 * sz.pieces
    u[sz.solid : end, 0 : sz.share] = value[64 : 64 + sz.tail]
    vec_out[5:6, 0:half_rows] = own_half(value[64 + sz.tail : 65 + sz.tail])
    tail_out = load(u.at[sz.solid : end, 0:512], out_down.at[sz.solid : end])
    theirs = rows_at(pair * at.c + block * (1 - at.d), block)

    def part_sum(side, lanes):
        result = jnp.zeros((block, sz.hidden), jnp.float32)
        for c in range(4):
            result = result + h2_t[rows_at(pair * c + block * side, block), lanes].astype(jnp.float32)
        return result

    every = slice(0, sz.hidden)
    gu[theirs] = part_sum(1 - at.d, every).astype(low)
    wires.copy(gu.at[theirs], xu, at.peer(4), 97)
    o_relay(relay_out)
    o_heads(3)
    res_across()
    mine_sum = part_sum(at.d, every)
    down_out.wait()
    tail_out.wait()
    wires.arrived(xu, 97, at.peer(4))
    partner_sum = xu[...].astype(jnp.float32)
    for side in range(2):

        @pl.when(at.d == side)
        def _():
            both = (mine_sum, partner_sum) if side == 0 else (partner_sum, mine_sum)
            for j in range(4):
                rows = slice(block * j, block * (j + 1))
                for i in range(2):
                    u[rows, half_rows * i : half_rows * (i + 1)] = both[i][:, half_rows * j : half_rows * (j + 1)]

    bias_sum = mine_sum[half_rows : half_rows + 1]
    for j in range(4):
        vec_out[8 + j : 9 + j, 0:half_rows] = bias_sum[:, half_rows * j : half_rows * (j + 1)]
    up_out = load(u.at[0 : 4 * block, 0:512], out_up)

    for c in range(4):
        o_arrived(c)
        needed = o_from(c)
        made = load(zo.at[c], wd.at[pair * c : pair * (c + 1), 0 : sz.mixed], needed)
        brought.append((needed, made))

        @pl.when(jnp.logical_not(needed))
        def _():
            wd[pair * c : pair * (c + 1), 0 : sz.mixed] = jnp.zeros((pair, sz.mixed), low)

    all_brought()
    value = xo[at.c].astype(jnp.float32)
    for c in range(4):
        value = value + wd[pair * c : pair * (c + 1), 0 : sz.mixed].astype(jnp.float32)
    flipped = natural_rows(value)
    vec_out[4:5, 0:half_rows] = own_half(flipped[half_rows : half_rows + 1])
    flipped = flipped[0:block]
    for i in range(4):
        held = (dk_sum, dv_sum)[i // 2].at[block * (i % 2) : block * (i % 2 + 1)]
        lanes = min(128, sz.share - 128 * i)
        held[:, 0:lanes] = flipped[:, 128 * i : 128 * i + lanes]
        stay.append(load(held, out_out.at[:, 128 * i : 128 * (i + 1)]))

    grad_across()

    for mask in range(1, 8):
        wires.arrived(va.at[mask], 84 + mask, at.peer(mask))
    vb[at.c] = functools.reduce(lambda a, b: a + b, [va[mask] for mask in range(8)])
    for c in range(4):
        wires.copy(vb.at[at.c], vb.at[at.c], at.along(c), 98 + at.c, at.c != c)

    for c in range(4):
        wires.arrived(vb.at[c], 98 + c, at.along(c), at.c != c)
    sums = vb[0] + vb[1] + vb[2] + vb[3]
    picked_sums = jnp.zeros((4, half_rows), jnp.float32)
    for i in range(8):
        cut = sums[0:4, block * i : block * i + half_rows]
        picked_sums = jnp.where(2 * at.c + at.d == i, cut, picked_sums)
    vec_out[0:4, 0:half_rows] = picked_sums
    res_finish()
    grad_finish()
    up_out.wait()
    rest_lanes = sz.heads - sz.solid
    for c in range(4):
        h_arrived(c)
        needed = h_from(c)
        rows = slice(block * c, block * (c + 1))
        parts = (
            load(zh.at[c, :, 0 : sz.solid], wd.at[rows], needed),
            load(zh.at[c, :, sz.solid : sz.heads], wu.at[rows, 0:rest_lanes], needed),
        )
        brought += [(needed, made) for made in parts]

        @pl.when(jnp.logical_not(needed))
        def _():
            wd[rows] = jnp.zeros((block, sz.solid), low)
            wu[rows, 0:rest_lanes] = jnp.zeros((block, rest_lanes), low)

    all_brought()
    left = xh[at.c, :, 0 : sz.solid].astype(jnp.float32)
    right = xh[at.c, :, sz.solid : sz.heads].astype(jnp.float32)
    for c in range(4):
        rows = slice(block * c, block * (c + 1))
        left = left + wd[rows].astype(jnp.float32)
        right = right + wu[rows, 0:rest_lanes].astype(jnp.float32)
    whole = jnp.concatenate([left, right], axis=1)
    for i in range(3):
        turned_columns = jnp.concatenate(
            [
                whole[:, main * i : main * (i + 1)],
                whole[:, 3 * main + slack * i : 3 * main + slack * (i + 1)],
            ],
            axis=1,
        )
        rows = slice(block * i, block * (i + 1))
        for r in range(4):

            @pl.when(at.r == r)
            def _():
                cut = slack * r
                value = turned_columns
                if cut:
                    value = jnp.concatenate([value[:, cut:], value[:, 0:cut]], axis=1)
                u[rows, 0 : sz.share] = value
                if i != 1:
                    vec_out[6 + i // 2 : 7 + i // 2, 0:half_rows] = own_half(
                        value[half_rows : half_rows + 1]
                    )

    stay.append(load(u.at[0 : 3 * block, 0:512], out_heads))
    for made in stay:
        made.wait()
    wires.close()


def update_kernel(sz, rates, grads, result_in, grad_in, weights, firsts, seconds, outs):
    down, out, up, heads, vectors = grads
    share, pieces, block = sz.share, sz.pieces, sz.block

    def move(i, place, gradient, decay):
        weight = weights[i][place]
        first_new = BETA_FIRST * firsts[i][place] + (1.0 - BETA_FIRST) * gradient
        second_new = BETA_SECOND * seconds[i][place] + (1.0 - BETA_SECOND) * (gradient * gradient)
        divisor = jnp.sqrt(second_new * (1.0 / (1.0 - BETA_SECOND**STEP))) + ADAM_EPSILON
        change = first_new * (rates[i] / (1.0 - BETA_FIRST**STEP)) / divisor
        weight_new = weight * (1.0 - rates[i] * decay) - change
        outs[3 * i + 2][place] = first_new
        outs[3 * i + 3][place] = second_new
        outs[3 * i + 4][place] = weight_new

    for part in range(3):
        move(0, part, heads[part, :, 0:share], MATRIX_DECAY)
    move(1, slice(None), out[:, 0:share], MATRIX_DECAY)
    move(2, slice(None), jnp.stack([up[j, :, 0:share] for j in range(4)], axis=1), MATRIX_DECAY)
    move(3, slice(None), down[:, 0:share], MATRIX_DECAY)

    @pl.when(pl.program_id(0) == 0)
    def _():
        for i, source, row in (
            (4, 0, 0), (4, 1, 1), (5, 4, 0), (5, 2, 1), (5, 3, 2), (5, 5, 3),
            (6, 6, 0), (6, 7, 1), (7, 8, 0), (7, 9, 1), (7, 10, 2), (7, 11, 3),
        ):
            move(i, row, vectors[source : source + 1, 0:pieces], 0.0)

    def plain(rows):
        rows = rows.astype(jnp.float32)
        return jnp.concatenate([rows[0:pieces], rows[block : block + pieces]], axis=0)

    @pl.when(pl.program_id(0) == 1)
    def _():
        outs[0][...] = plain(result_in[...]).astype(jnp.bfloat16)

    @pl.when(pl.program_id(0) == 2)
    def _():
        outs[1][...] = plain(grad_in[...])


def fused(
    tokens,
    cotangent,
    segments,
    weights,
    firsts,
    seconds,
):
    low = jnp.bfloat16
    seq, share = tokens.shape
    pieces = weights[1].shape[2]
    sz = Sizes(share, pieces, seq)
    block, main = sz.block, sz.main

    def views(arrays):
        heads, out, up, down, *small = arrays
        return (
            jnp.transpose(heads.reshape(pieces, 3, share), (1, 0, 2)),
            out.reshape(pieces, share),
            up.reshape(pieces, 4, share),
            down.reshape(4 * pieces, share),
            *[each.reshape(each.shape[0], 1, pieces) for each in small],
        )

    viewed = views(weights)
    labels = segments.reshape(1, -1)

    def made(*shape, dtype=low):
        return jax.ShapeDtypeStruct(shape, dtype)

    def held(*shape, dtype=low):
        return pltpu.VMEM(shape, dtype)

    w, seq, both, part = sz.width, sz.seq, sz.both, sz.part
    vmem, anywhere = pl.BlockSpec(memory_space=pltpu.VMEM), pl.BlockSpec(memory_space=pl.ANY)
    dma = pltpu.SemaphoreType.DMA
    f32 = jnp.float32
    wide = 3 * 128 + 128
    outs = pl.pallas_call(
        functools.partial(forward_kernel, sz),
        out_shape=(
            made(w, sz.heads),
            made(w, 2 * sz.mixed),
            made(w, sz.hidden),
            made(w, sz.solid),
            made(w, seq),
            made(w, both),
            made(w, sz.solid),
            made(w, 128),
            made(both, w),
            made(both, sz.hidden, dtype=f32),
            made(both, sz.hidden),
            made(seq, main + 128),
            made(seq, main + 128),
            made(seq, main + 128),
            made(seq, 2 * sz.mixed),
            made(seq, 128, dtype=f32),
            made(part, w, dtype=f32),
            made(part, w),
            made(8, w, dtype=f32),
        ),
        in_specs=[anywhere] * 6 + [vmem] * 5,
        out_specs=[anywhere] * 19,
        scratch_shapes=[
            held(w, sz.heads),
            held(w, 2 * sz.mixed),
            held(w, sz.hidden),
            held(w, sz.solid),
            held(w, seq),
            held(w, both),
            held(w, sz.solid),
            held(w, 128),
            held(w, both),
            held(both, w),
            held(both, sz.hidden, dtype=f32),
            held(both, sz.hidden),
            held(seq, main + 128),
            held(seq, main + 128),
            held(seq, main + 128),
            held(seq, 2 * sz.mixed),
            held(seq, 128, dtype=f32),
            held(part, w, dtype=f32),
            held(part, w),
            held(8, w, dtype=f32),
            held(w, seq),
            held(seq, w),
            held(both, w),
            held(seq, sz.heads),
            held(seq, main + 128),
            held(w, 128),
            held(seq, w),
            held(seq, 256),
            held(seq, 256),
            held(seq, 128),
            held(2, part, w),
            held(1, part, w),
            held(1, part, w),
            held(share, seq),
            held(share, seq),
            held(3, pieces, share, dtype=f32),
            held(pieces, share, dtype=f32),
            held(pieces, 4, share, dtype=f32),
            held(4 * pieces, share, dtype=f32),
            held(sz.pair, seq),
            held(sz.pair, seq),
            held(block, sz.hidden),
            held(sz.pair, 128),
            held(seq, 1, dtype=f32),
            held(block, seq),
            held(block, seq),
            dma((160,)),
            dma((160,)),
            dma((48,)),
        ],
        compiler_params=pltpu.CompilerParams(
            collective_id=0, has_side_effects=True, vmem_limit_bytes=VMEM_BYTES
        ),
        cost_estimate=pl.CostEstimate(flops=10**10, bytes_accessed=10**8, transcendentals=10**6),
    )(tokens.T, cotangent.T, *viewed, labels)
    (wh, wo, wu, wd, h1_t, h2_t, gd, gt, dy, u, gl, qw, kw, vw, a_nat, lse, x2, x_own, vec_rows) = outs
    outs = pl.pallas_call(
        functools.partial(backward_kernel, sz),
        out_shape=(
            made(4 * pieces, 512, dtype=f32),
            made(4 * block, 512, dtype=f32),
            made(block, 512, dtype=f32),
            made(3 * block, 512, dtype=f32),
            made(sz.pair, seq),
            made(sz.pair, seq),
            made(16, 256, dtype=f32),
            made(4, sz.pair, sz.solid),
            made(4, sz.pair, sz.hidden),
            made(4, sz.pair, sz.mixed),
            made(4, block, sz.heads),
            made(4, block, seq),
            made(2, block, seq),
            made(4, block, seq),
            made(2, block, seq),
        ),
        in_specs=[anywhere] * 18 + [vmem] * 2,
        out_specs=[anywhere] * 6 + [vmem] + [anywhere] * 8,
        scratch_shapes=[
            held(sz.pair, sz.solid),
            held(sz.pair, sz.hidden),
            held(sz.pair, sz.mixed),
            held(block, sz.heads),
            held(seq, main + 128),
            held(seq, main + 128),
            held(seq, main + 128),
            held(seq, 2 * sz.mixed),
            held(seq, 128, dtype=f32),
            held(part, w, dtype=f32),
            held(part, w),
            held(block, sz.hidden),
            held(both, w),
            held(w, both),
            held(both, sz.hidden, dtype=f32),
            held(both, sz.hidden),
            held(w, both),
            held(w, sz.solid),
            held(w, sz.hidden),
            held(w, 2 * sz.mixed),
            held(w, sz.heads),
            held(w, 128),
            held(part, w),
            held(both, sz.hidden),
            held(w, sz.heads),
            held(w, sz.hidden),
            held(w, 2 * sz.mixed),
            held(4, block, sz.heads),
            held(4, sz.pair, sz.mixed),
            held(4, part, w),
            held(3, part, w),
            held(4, part, w),
            held(3, part, w),
            held(2, part, w),
            held(1, part, w),
            held(3, part, w),
            held(seq, w),
            held(seq, 2 * sz.mixed),
            held(seq, 128, dtype=f32),
            held(seq, 128, dtype=f32),
            held(part, w, dtype=f32),
            held(seq, 256),
            held(seq, 256),
            held(seq, 128),
            held(seq, 128),
            held(seq, 1, dtype=f32),
            held(4, 2, block, part),
            held(4, 2, block, part),
            held(8, 8, w, dtype=f32),
            held(4, 8, w, dtype=f32),
            dma((128,)),
            dma((120,)),
            dma((80,)),
        ],
        compiler_params=pltpu.CompilerParams(
            collective_id=1, has_side_effects=True, vmem_limit_bytes=VMEM_BYTES
        ),
        cost_estimate=pl.CostEstimate(flops=2 * 10**10, bytes_accessed=10**8, transcendentals=10**6),
    )(
        dy, gd, gt, u, gl, h2_t, wd, wu, wo, wh, h1_t,
        qw, kw, vw, a_nat, lse, x2, x_own, vec_rows, labels,
    )
    down, up, out, heads, result_home, grad_home, vectors = outs[:7]
    steps = 5
    chunk = pieces // steps

    def rows_of(shape, axis, size):
        block_shape = list(shape)
        block_shape[axis] = size
        return pl.BlockSpec(tuple(block_shape), lambda i: tuple(i if a == axis else 0 for a in range(len(shape))))

    def whole(shape):
        return pl.BlockSpec(tuple(shape), lambda i: (0,) * len(shape))

    matrix_specs = (
        rows_of((3, pieces, share), 1, chunk),
        rows_of((pieces, share), 0, chunk),
        rows_of((pieces, 4, share), 0, chunk),
        rows_of((4 * pieces, share), 0, 4 * chunk),
        *[whole(each.shape) for each in viewed[4:]],
    )
    grads = (down, out, up.reshape(4, block, 512), heads.reshape(3, block, 512), vectors)
    grad_specs = (
        rows_of((4 * pieces, 512), 0, 4 * chunk),
        rows_of((block, 512), 0, chunk),
        rows_of((4, block, 512), 1, chunk),
        rows_of((3, block, 512), 1, chunk),
        whole((16, 256)),
    )
    rates = (0.05, 0.2, 0.05, 0.025, 0.3, 0.3, 0.3, 0.3)
    arguments = (*grads, result_home, grad_home, *viewed, *views(firsts), *views(seconds))
    out_shape = [made(share, seq), made(share, seq, dtype=f32)]
    out_specs = [whole((share, seq)), whole((share, seq))]
    for each, spec in zip(viewed, matrix_specs, strict=True):
        out_shape += [jax.ShapeDtypeStruct(each.shape, f32)] * 3
        out_specs += [spec] * 3

    def update(*refs):
        ins, outs = refs[:31], refs[31:]
        update_kernel(sz, rates, ins[:5], ins[5], ins[6], ins[7:15], ins[15:23], ins[23:31], outs)

    updated = pl.pallas_call(
        update,
        grid=(steps,),
        out_shape=out_shape,
        in_specs=[*grad_specs, whole((sz.pair, seq)), whole((sz.pair, seq)), *matrix_specs * 3],
        out_specs=out_specs,
        compiler_params=pltpu.CompilerParams(vmem_limit_bytes=VMEM_BYTES),
        cost_estimate=pl.CostEstimate(
            flops=20 * 10**6, bytes_accessed=30 * 10**6, transcendentals=2 * 10**6
        ),
    )(*arguments)
    results = [updated[0].T, updated[1].T]
    for i, weight in enumerate(weights):
        for each in updated[2 + 3 * i : 5 + 3 * i]:
            if i == 0:
                each = jnp.transpose(each, (1, 0, 2))
            results.append(each.reshape(weight.shape))
    return tuple(results)


def normalize(inputs):
    center = jnp.mean(inputs, axis=1, keepdims=True)
    spread = jnp.mean(inputs * inputs, axis=1, keepdims=True) - center * center
    inverse = lax.rsqrt(spread + NORM_EPSILON)
    return ((inputs - center) * inverse, inverse)


def norm_pull(upstream, centered, inverse, gain):
    scaled = upstream * gain
    inner = (
        scaled
        - jnp.mean(scaled, axis=1, keepdims=True)
        - centered * jnp.mean(scaled * centered, axis=1, keepdims=True)
    )
    return inner * inverse


def crossed(blocks, n):
    pairs = [(i * n + j, j * n + i) for i in range(n) for j in range(n)]
    return lax.ppermute(blocks, ("row", "col"), pairs)


def scatter_rows(partial):
    return lax.psum_scatter(
        partial.astype(jnp.bfloat16), "row", scatter_dimension=0, tiled=True
    ).astype(jnp.float32)


def gather_rows(local):
    return lax.all_gather(local, "row", axis=0, tiled=True)


def split_heads(rows):
    return jnp.transpose(rows.reshape(rows.shape[0], -1, HD), (1, 0, 2))


def join_heads(values):
    return jnp.transpose(values, (1, 0, 2)).reshape(values.shape[1], -1)


def scores_of(queries, keys, allowed):
    scores = jnp.einsum(
        "hqe,hke->hqk", queries, keys, preferred_element_type=jnp.float32
    ) * HD ** (-0.5)
    return jnp.where(allowed[None], scores, MASKED)


def gathered(
    tokens,
    cotangent,
    segments,
    w_heads,
    w_out,
    w_up,
    w_down,
    norm_vectors,
    width_vectors,
    attend_bias,
    hidden_vectors,
):
    n_dp, n_row, n_col = (lax.axis_size(name) for name in ("dp", "row", "col"))
    row = lax.axis_index("row")
    low = jnp.bfloat16
    share = tokens.shape[1]
    width = share * n_col
    seq = tokens.shape[0]
    part = seq // n_row
    near = HEADS // n_row
    window = (HEADS - near * (n_row - 1)) * HD
    step = near * HD
    edge = width - (share + step * (n_row - 1)) if n_row > 1 else 0
    edge = window - share
    to_next = [(i, i + 1) for i in range(n_row - 1)]
    to_last = [(i + 1, i) for i in range(n_row - 1)]
    offset = edge - (share - step) * row

    vectors = jnp.concatenate(
        [
            norm_vectors.reshape(2, -1),
            width_vectors.reshape(4, -1),
            attend_bias.reshape(2, -1),
            hidden_vectors.reshape(4, -1),
        ]
    ).astype(low)
    vectors = lax.all_gather(vectors, ("row", "col", "dp"), axis=0, tiled=False)
    vectors = vectors.reshape(n_row, n_col, n_dp, 12, -1).astype(jnp.float32)
    by_col = jnp.transpose(vectors[0], (2, 0, 1, 3)).reshape(12, width)
    by_row = jnp.transpose(vectors[:, 0], (2, 0, 1, 3)).reshape(12, width)
    gain_one, shift_one, bias_out, gain_two, shift_two, bias_down = (by_col[i] for i in range(6))
    zeros = jnp.zeros((1, window), jnp.float32)
    attend_rows = lax.dynamic_slice_in_dim(by_row[6:8], row * step, window, axis=1)
    heads_bias = jnp.concatenate([attend_rows[0:1], zeros, attend_rows[1:2]]).reshape(-1)
    unit_bias = lax.dynamic_slice_in_dim(by_row[8:12], row * share, share, axis=1).reshape(-1)

    own = w_heads.astype(low).reshape(-1, 3, share)
    passed = lax.ppermute(own[:, :, share - edge :], "row", to_next)
    own = jnp.concatenate([passed, own, jnp.zeros_like(passed)], axis=2)
    own = lax.dynamic_slice_in_dim(own, offset, window, axis=2).reshape(-1, 3 * window)
    heads_matrix = lax.all_gather(own, ("col", "dp"), axis=0, tiled=True)
    out_matrix = lax.all_gather(w_out.astype(low).reshape(-1, share), ("col", "dp"), axis=0)
    out_matrix = jnp.transpose(out_matrix.reshape(n_col, share, share), (1, 0, 2))
    out_matrix = out_matrix.reshape(share, width)
    passed = lax.ppermute(out_matrix[share - edge :], "row", to_next)
    out_matrix = jnp.concatenate([passed, out_matrix, jnp.zeros_like(passed)])
    out_matrix = lax.dynamic_slice_in_dim(out_matrix, offset, window)
    owned = (jnp.arange(window) < step) | (row == n_row - 1)
    out_matrix = jnp.where(owned[:, None], out_matrix, jnp.zeros_like(out_matrix))
    up_matrix = lax.all_gather(
        w_up.astype(low).reshape(-1, 4 * share), ("col", "dp"), axis=0, tiled=True
    )
    down_matrix = lax.all_gather(w_down.astype(low).reshape(4, -1, share), ("col", "dp"), axis=0)
    down_matrix = down_matrix.reshape(n_col, n_dp, 4, -1, share)
    down_matrix = jnp.transpose(down_matrix, (2, 1, 3, 0, 4)).reshape(4 * share, width)

    inputs_low = lax.all_gather(crossed(tokens, n_row), "row", axis=1, tiled=True)
    upstream = lax.all_gather(crossed(cotangent, n_row), "row", axis=1, tiled=True)
    inputs = inputs_low.astype(jnp.float32)
    centered_one, inverse_one = normalize(inputs)
    normed_one = (centered_one * gain_one + shift_one).astype(low)
    projected = (times(normed_one, heads_matrix) + heads_bias).astype(low)
    queries, keys, values = (
        split_heads(projected[:, i * window : (i + 1) * window]) for i in range(3)
    )
    labels = lax.dynamic_slice_in_dim(segments, lax.axis_index("col") * seq, seq)
    places = jnp.arange(seq, dtype=jnp.int32)
    allowed = (labels[:, None] == labels[None, :]) & (places[:, None] >= places[None, :])
    scores = scores_of(queries, keys, allowed)
    highest = jnp.max(scores, axis=-1, keepdims=True)
    log_total = highest + jnp.log(jnp.sum(jnp.exp(scores - highest), axis=-1, keepdims=True))
    soft = jnp.exp(scores - log_total).astype(low)
    mixed = jnp.einsum("hqk,hke->hqe", soft, values, preferred_element_type=jnp.float32)
    mixed = join_heads(mixed.astype(low))
    branch = scatter_rows(times(mixed, out_matrix))
    mine = row * part
    middle = lax.dynamic_slice_in_dim(inputs, mine, part) + (branch + bias_out)
    centered_two, inverse_two = normalize(middle)
    normed_two = gather_rows((centered_two * gain_two + shift_two).astype(low))
    hidden = times(normed_two, up_matrix) + unit_bias
    activated, smooth_pull = jax.vjp(smooth, hidden)
    activated = activated.astype(low)
    result = (middle + (scatter_rows(times(activated, down_matrix)) + bias_down)).astype(low)

    down_back = times_flipped(upstream, down_matrix)
    grad_down = times_outer(activated, upstream)
    hidden_back = smooth_pull(down_back)[0].astype(low)
    grad_up = times_outer(normed_two, hidden_back)
    unit_sum = jnp.sum(hidden_back, axis=0, dtype=jnp.float32)
    normed_two_back = scatter_rows(times_flipped(hidden_back, up_matrix))
    upstream_own = lax.dynamic_slice_in_dim(upstream, mine, part).astype(jnp.float32)
    middle_back = upstream_own + norm_pull(normed_two_back, centered_two, inverse_two, gain_two)
    branch_own = middle_back.astype(low)
    branch_back = gather_rows(branch_own)
    mixed_back = times_flipped(branch_back, out_matrix).astype(low)
    grad_out = times_outer(mixed, branch_back)
    mixed_back = split_heads(mixed_back)
    scores_again = scores_of(queries, keys, allowed)
    soft = jnp.exp(scores_again - log_total)
    soft_back = jnp.einsum("hqe,hke->hqk", mixed_back, values, preferred_element_type=jnp.float32)
    row_inner = jnp.sum(soft_back * soft, axis=-1, keepdims=True)
    score_back = (soft * (soft_back - row_inner)).astype(low)
    query_back = jnp.einsum(
        "hqk,hke->hqe", score_back, keys, preferred_element_type=jnp.float32
    ) * HD ** (-0.5)
    key_back = jnp.einsum(
        "hqk,hqe->hke", score_back, queries, preferred_element_type=jnp.float32
    ) * HD ** (-0.5)
    value_back = jnp.einsum(
        "hqk,hqe->hke", soft.astype(low), mixed_back, preferred_element_type=jnp.float32
    )
    heads_back = jnp.concatenate(
        [join_heads(each.astype(low)) for each in (query_back, key_back, value_back)], axis=1
    )
    heads_sum = jnp.sum(heads_back, axis=0, dtype=jnp.float32)
    normed_one_back = scatter_rows(times_flipped(heads_back, heads_matrix))
    grad_heads = times_outer(normed_one, heads_back)
    centered_own = lax.dynamic_slice_in_dim(centered_one, mine, part)
    inverse_own = lax.dynamic_slice_in_dim(inverse_one, mine, part)
    input_back = middle_back + norm_pull(normed_one_back, centered_own, inverse_own, gain_one)

    def homeward(own):
        own = lax.all_to_all(own, "row", split_axis=1, concat_axis=0, tiled=True)
        return crossed(own, n_row)

    result_tokens = homeward(result)
    input_gradient = homeward(input_back.astype(low)).astype(jnp.float32)

    by_token = jnp.stack(
        [
            jnp.sum(normed_one_back * centered_own, axis=0),
            jnp.sum(normed_one_back, axis=0),
            jnp.sum(branch_own.astype(jnp.float32), axis=0),
            jnp.sum(normed_two_back * centered_two, axis=0),
            jnp.sum(normed_two_back, axis=0),
            jnp.sum(upstream_own, axis=0),
        ]
    )
    owned_rows = jnp.where(owned, heads_sum.reshape(3, window)[0::2], 0.0)
    by_unit = jnp.concatenate(
        [
            lax.dynamic_update_slice_in_dim(
                jnp.zeros((2, width), jnp.float32), owned_rows, row * step, axis=1
            ),
            lax.dynamic_update_slice_in_dim(
                jnp.zeros((4, width), jnp.float32), unit_sum.reshape(4, share), row * share, axis=1
            ),
        ]
    )
    sums = lax.psum(jnp.concatenate([by_token, by_unit]), ("dp", "row", "col"))
    pieces = share // n_dp
    inner = lax.axis_index("dp") * pieces
    col_sums = lax.dynamic_slice_in_dim(sums, lax.axis_index("col") * share + inner, pieces, axis=1)
    row_sums = lax.dynamic_slice_in_dim(sums, row * share + inner, pieces, axis=1)

    both = ("col", "dp")

    def to_owner(gradient):
        return lax.psum_scatter(gradient, both, scatter_dimension=0, tiled=True)

    got_heads = to_owner(grad_heads.astype(low)).reshape(pieces, 3, window)
    got_heads = jnp.where(owned, got_heads, jnp.zeros_like(got_heads))
    passed = lax.ppermute(got_heads[:, :, :edge], "row", to_last)
    got_heads = jnp.concatenate([got_heads, jnp.zeros_like(passed)], axis=2)
    got_heads = lax.dynamic_slice_in_dim(got_heads, edge - offset, share, axis=2)
    passed = jnp.concatenate([jnp.zeros((pieces, 3, share), low), passed, jnp.zeros_like(passed)], axis=2)
    got_heads = got_heads + lax.dynamic_slice_in_dim(passed, share - step + edge - offset, share, axis=2)
    low_out = jnp.where(owned[:, None], grad_out, 0.0).astype(low)
    passed = lax.ppermute(low_out[:edge], "row", to_last)
    low_out = jnp.concatenate([low_out, jnp.zeros_like(passed)])
    low_out = lax.dynamic_slice_in_dim(low_out, edge - offset, share)
    passed = jnp.concatenate([jnp.zeros((share, width), low), passed, jnp.zeros_like(passed)])
    low_out = low_out + lax.dynamic_slice_in_dim(passed, share - step + edge - offset, share)
    low_out = jnp.transpose(low_out.reshape(n_dp, pieces, n_col, share), (2, 0, 1, 3))
    got_out = to_owner(low_out.reshape(-1, share))
    got_up = to_owner(grad_up.astype(low))
    low_down = grad_down.astype(low).reshape(4, n_dp, pieces, n_col, share)
    low_down = jnp.transpose(low_down, (3, 1, 0, 2, 4)).reshape(-1, share)
    got_down = to_owner(low_down)

    reduced = [
        each.astype(jnp.float32).reshape(like.shape)
        for each, like in (
            (got_heads, w_heads),
            (got_out, w_out),
            (got_up, w_up),
            (got_down, w_down),
            (col_sums[0:2], norm_vectors),
            (col_sums[2:6], width_vectors),
            (row_sums[6:8], attend_bias),
            (row_sums[8:12], hidden_vectors),
        )
    ]
    return result_tokens, input_gradient, reduced


def per_device(
    tokens,
    cotangent,
    segments,
    w_heads,
    w_out,
    w_up,
    w_down,
    norm_vectors,
    width_vectors,
    attend_bias,
    hidden_vectors,
    drift_heads,
    drift_out,
    drift_up,
    drift_down,
    drift_norm,
    drift_width,
    drift_attend,
    drift_hidden,
    power_heads,
    power_out,
    power_up,
    power_down,
    power_norm,
    power_width,
    power_attend,
    power_hidden,
):
    weights = (
        w_heads,
        w_out,
        w_up,
        w_down,
        norm_vectors,
        width_vectors,
        attend_bias,
        hidden_vectors,
    )
    firsts = (
        drift_heads,
        drift_out,
        drift_up,
        drift_down,
        drift_norm,
        drift_width,
        drift_attend,
        drift_hidden,
    )
    seconds = (
        power_heads,
        power_out,
        power_up,
        power_down,
        power_norm,
        power_width,
        power_attend,
        power_hidden,
    )
    sizes = tuple(lax.axis_size(name) for name in ("dp", "row", "col"))
    if sizes == (2, 4, 4):
        return fused(tokens, cotangent, segments, weights, firsts, seconds)
    result_tokens, input_gradient, reduced = gathered(tokens, cotangent, segments, *weights)
    heads_up = adam(w_heads, reduced[0], drift_heads, power_heads, 0.05, MATRIX_DECAY)
    out_up = adam(w_out, reduced[1], drift_out, power_out, 0.2, MATRIX_DECAY)
    up_up = adam(w_up, reduced[2], drift_up, power_up, 0.05, MATRIX_DECAY)
    down_up = adam(w_down, reduced[3], drift_down, power_down, 0.025, MATRIX_DECAY)
    norm_up = adam(norm_vectors, reduced[4], drift_norm, power_norm, 0.3, 0.0)
    width_up = adam(width_vectors, reduced[5], drift_width, power_width, 0.3, 0.0)
    attend_up = adam(attend_bias, reduced[6], drift_attend, power_attend, 0.3, 0.0)
    hidden_up = adam(hidden_vectors, reduced[7], drift_hidden, power_hidden, 0.3, 0.0)
    return (
        result_tokens,
        input_gradient,
        heads_up[0],
        heads_up[1],
        heads_up[2],
        out_up[0],
        out_up[1],
        out_up[2],
        up_up[0],
        up_up[1],
        up_up[2],
        down_up[0],
        down_up[1],
        down_up[2],
        norm_up[0],
        norm_up[1],
        norm_up[2],
        width_up[0],
        width_up[1],
        width_up[2],
        attend_up[0],
        attend_up[1],
        attend_up[2],
        hidden_up[0],
        hidden_up[1],
        hidden_up[2],
    )


def solution(mesh):
    return jax.shard_map(
        per_device,
        mesh=mesh,
        in_specs=(
            P(("dp", "row"), "col"),
            P(("dp", "row"), "col"),
            P("dp"),
            P("col", "dp", None, None, "row"),
            P("row", "dp", None, "col"),
            P("col", "dp", None, None, "row"),
            P(None, "row", "dp", None, "col"),
            P(None, "col", "dp", None),
            P(None, "col", "dp", None),
            P(None, "row", "dp", None),
            P(None, "row", "dp", None),
            P("col", "dp", None, None, "row"),
            P("row", "dp", None, "col"),
            P("col", "dp", None, None, "row"),
            P(None, "row", "dp", None, "col"),
            P(None, "col", "dp", None),
            P(None, "col", "dp", None),
            P(None, "row", "dp", None),
            P(None, "row", "dp", None),
            P("col", "dp", None, None, "row"),
            P("row", "dp", None, "col"),
            P("col", "dp", None, None, "row"),
            P(None, "row", "dp", None, "col"),
            P(None, "col", "dp", None),
            P(None, "col", "dp", None),
            P(None, "row", "dp", None),
            P(None, "row", "dp", None),
        ),
        out_specs=(
            P(("dp", "row"), "col"),
            P(("dp", "row"), "col"),
            P("col", "dp", None, None, "row"),
            P("col", "dp", None, None, "row"),
            P("col", "dp", None, None, "row"),
            P("row", "dp", None, "col"),
            P("row", "dp", None, "col"),
            P("row", "dp", None, "col"),
            P("col", "dp", None, None, "row"),
            P("col", "dp", None, None, "row"),
            P("col", "dp", None, None, "row"),
            P(None, "row", "dp", None, "col"),
            P(None, "row", "dp", None, "col"),
            P(None, "row", "dp", None, "col"),
            P(None, "col", "dp", None),
            P(None, "col", "dp", None),
            P(None, "col", "dp", None),
            P(None, "col", "dp", None),
            P(None, "col", "dp", None),
            P(None, "col", "dp", None),
            P(None, "row", "dp", None),
            P(None, "row", "dp", None),
            P(None, "row", "dp", None),
            P(None, "row", "dp", None),
            P(None, "row", "dp", None),
            P(None, "row", "dp", None),
        ),
        check_vma=False,
    )
```

profile of v0, /device:TPU:5, one launch (start us, length us, event | category | flops | bytes accessed | tf_op | source)
XLA Modules:
  0.0 401.1 jit_solution(8560948297443840627)
XLA Ops:
  0.7 196.7 %shard_map.458 = (bf16[1664,1280]{1,0:T(8,128)(2,1)}, bf16[1664,512]{1,0:T(8,128)(2,1)}, bf16[1664,896]{1,0:T(8,128)(2,1)}, bf16[1664,768]{1,0:T(8,128)(2,1)}, b...) custom-call(bf16[400,512]{1,0:T(8,128)(2,1)} %bitcast.141, ...), custom_call_target="tpu_custom_call" | custom-call | flops 10000000000 | bytes 100000000 | tf_op jit(solution)/shard_map/pallas_call | solution.py:1636
  197.4 186.5 %shard_map.459 = (f32[800,512]{1,0:T(8,128)}, f32[832,512]{1,0:T(8,128)}, f32[208,512]{1,0:T(8,128)}, f32[624,512]{1,0:T(8,128)}, bf16[416,512]{1,0:T(8,128)(2,1...) custom-call(bf16[1024,1664]{1,0:T(8,128)(2,1)} %get-tuple-element.78, ...), custom_call_target="tpu_custom_call" | custom-call | flops 20000000000 | bytes 100000000 | tf_op jit(solution)/shard_map/pallas_call | solution.py:1718
  383.9 16.7 %shard_map.460 = (bf16[400,512]{1,0:T(8,128)(2,1)}, f32[400,512]{1,0:T(8,128)}, f32[3,200,400]{2,1,0:T(8,128)}, f32[3,200,400]{2,1,0:T(8,128)}, f32[3,200,400]{2...) custom-call(f32[800,512]{1,0:T(8,128)} %get-tuple-element.97.refs_0_, ...), custom_call_target="tpu_custom_call" | custom-call | flops 20000000 | bytes 30000000 | tf_op jit(solution)/shard_map/pallas_call | solution.py:1841
where the time goes:
time: 407 us; the launch traced here: 401 us
  Pallas kernels  400 us (98%)
    pallas_call x1, Pallas kernels, fused(): pl.pallas_call(functools.partial(forward_kernel, sz), out_shape=(made(w,...  197 us
    pallas_call x1, Pallas kernels, fused(): pl.pallas_call(functools.partial(backward_kernel, sz), out_shape=(made(4...  186 us
    pallas_call x1, Pallas kernels, fused(): pl.pallas_call(update, grid=(steps,), out_shape=out_shape, in_specs=[*gra...  16.7 us

commit v1 on v0

--- a/solution.py
+++ b/solution.py
@@ -470,7 +470,8 @@
         )
     ):
         fetched.append(pltpu.make_async_copy(source, target, locals_.at[40 + i]))
-        fetched[i].start()
+    for made in fetched[0:2]:
+        made.start()
     row_labels = segments.at[:, lanes_at(sz.seq * at.c, sz.seq)]
 
     def halves(value, target):
@@ -503,6 +504,8 @@
     vec[own_rows] = jnp.where(carrier, 1.0, flat).T[0:block].astype(low)
     fetched[0].wait()
     halves(x_raw[...], x_home)
+    for made in fetched[2:6]:
+        made.start()
     greet(at, False)
 
     def x_piece(c, d, y):
@@ -736,9 +739,6 @@
             needed = needed & (at.c != 1)
         wires.arrived(wo_block(at.d)(c), 28 + c, at.along(c), needed)
         wires.copy(wo_block(at.d)(c), wo_block(at.d)(c), at.peer(4), 32 + c, at.c != c)
-
-    dy_crossed()
-    dy_done = share_pieces(wires, (2, 4, 6), dy_piece, at, 124)
 
     half = sz.seq // 2
 
@@ -787,6 +787,8 @@
         wd_first_send(distance)
         wd_second_send(distance)
     wires.arrived(edge_back, 53, (at.d, at.r + 1, at.c), at.r < 3)
+    dy_crossed()
+    dy_done = share_pieces(wires, (2, 4, 6), dy_piece, at, 124)
 
     def natural(column):
         inner = column % sz.mixed
@@ -821,7 +823,6 @@
     onward()
     wu_first()
     wu_second()
-    dy_done()
     middle = x_own[...].astype(jnp.float32) + total()
     x2[...] = middle
     flush(x2, x2_out)
@@ -833,6 +834,8 @@
     h2_done, _ = gather_group(
         wires, (2, 4, 6), lambda d, r: h2.at[rows_at(sz.part * (4 * d + r), sz.part)], at, 72
     )
+    dy_done()
+
     @pl.loop(0, sz.tiles)
     def _(i):
         dy[:, lanes_at(128 * i, 128)] = turned(dy_t[rows_at(128 * i, 128)]).astype(low)
@@ -991,30 +994,34 @@
 
     own_rows = rows_at(sz.part * (4 * at.d + at.r), sz.part)
     gd = gw.at[:, 0 : sz.solid]
-    loads = [
-        load(s, t)
-        for s, t in (
-            (dy_all, dy),
-            (wd_all, wd),
-            (u_all, u),
-            (dy_all.at[own_rows], dy_own),
-            (wu_all, wu),
-            (h2_t_all, h2_t),
-            (gl_all, gl),
-            (gd_all, gd),
-            (wo_all, wo),
-            (wh_all, wh),
-            (x2_all, x2),
-            (a_nat_all, a_nat),
-            (qw_all, qw),
-            (kw_all, kw),
-            (vw_all, vw),
-            (lse_all, lse),
-            (x_own_all, x_own),
-            (h1_t_all, dy_t.at[:, 0 : sz.seq]),
-            (gt_all, gt),
-        )
-    ]
+    wanted = (
+        (dy_all, dy),
+        (wd_all, wd),
+        (u_all, u),
+        (dy_all.at[own_rows], dy_own),
+        (wu_all, wu),
+        (h2_t_all, h2_t),
+        (gl_all, gl),
+        (gd_all, gd),
+        (wo_all, wo),
+        (wh_all, wh),
+        (x2_all, x2),
+        (a_nat_all, a_nat),
+        (qw_all, qw),
+        (kw_all, kw),
+        (vw_all, vw),
+        (lse_all, lse),
+        (x_own_all, x_own),
+        (h1_t_all, dy_t.at[:, 0 : sz.seq]),
+        (gt_all, gt),
+    )
+    loads = {}
+
+    def begin(*which):
+        for i in which:
+            loads[i] = load(*wanted[i])
+
+    begin(0, 1, 2)
     greet(at, False)
     stay = []
 
@@ -1037,13 +1044,15 @@
 
         return add
 
-    for made in (*loads[0:3], loads[4]):
-        made.wait()
+    for i in range(3):
+        loads[i].wait()
+    begin(4, 5, 18)
 
     def through(start, tile):
         lanes = lanes_at(start, tile)
         last = isinstance(start, int)
         if last:
+            loads[4].wait()
             upstream = pltpu.roll(times(dy[...], wu[:, lanes]), 64, 1)
         else:
             upstream = times(dy[...], wd[:, lanes])
@@ -1063,6 +1072,7 @@
         dy[:, lanes_at(start, tile)] = times_flipped(du[...], wu[rows_at(start, tile)]).astype(low)
 
     over_tiles(sz.width, back_up)
+    begin(3, 10, 7, 6, 8, 11, 12, 13, 14, 15, 16, 9, 17)
 
     def chunk_both(d, r):
         return sz.part * (4 * d + r)
@@ -1177,8 +1187,8 @@
 
     row_labels = segments.at[:, lanes_at(sz.seq * at.c, sz.seq)]
     col_labels[...] = jnp.concatenate([row_labels[...]] * 8, axis=0).astype(jnp.float32).T[:, 0:1]
-    for made in loads[12:17]:
-        made.wait()
+    for i in range(12, 17):
+        loads[i].wait()
     half = sz.seq // 2
     dqw, dkw = (du.at[sz.seq * i : sz.seq * (i + 1), 0 : main + 128] for i in range(2))
     dvw = gl.at[0 : sz.seq, 0 : main + 128]
@@ -1327,8 +1337,7 @@
         xh[there] = (gw[mine].astype(jnp.float32) + xh[there].astype(jnp.float32)).astype(low)
         h_send(step)
 
-    for made in loads[9:10]:
-        made.wait()
+    loads[9].wait()
 
     def back_in(start, tile):
         out = times_flipped(own_back[...], wh[rows_at(start, tile)])

time: 407 us -> 409 us (level)
    pallas_call x1, Pallas kernels: 186 us -> 191 us  [fused(): pl.pallas_call(functools.partial(backward_kernel, sz), out_shape=(made(4...]
where the time goes in v1:
time: 409 us; the launch traced here: 403 us
  Pallas kernels  402 us (98%)
    pallas_call x1, Pallas kernels, fused(): pl.pallas_call(functools.partial(forward_kernel, sz), out_shape=(made(w,...  194 us
    pallas_call x1, Pallas kernels, fused(): pl.pallas_call(functools.partial(backward_kernel, sz), out_shape=(made(4...  191 us
    pallas_call x1, Pallas kernels, fused(): pl.pallas_call(update, grid=(steps,), out_shape=out_shape, in_specs=[*gra...  16.7 us

profile of v1, /device:TPU:5, one launch (start us, length us, event | category | flops | bytes accessed | tf_op | source)
XLA Modules:
  0.0 402.8 jit_solution(6839982472977361528)
XLA Ops:
  0.7 194.1 %shard_map.458 = (bf16[1664,1280]{1,0:T(8,128)(2,1)}, bf16[1664,512]{1,0:T(8,128)(2,1)}, bf16[1664,896]{1,0:T(8,128)(2,1)}, bf16[1664,768]{1,0:T(8,128)(2,1)}, b...) custom-call(bf16[400,512]{1,0:T(8,128)(2,1)} %bitcast.141, ...), custom_call_target="tpu_custom_call" | custom-call | flops 10000000000 | bytes 100000000 | tf_op jit(solution)/shard_map/pallas_call | solution.py:1645
  194.8 190.8 %shard_map.459 = (f32[800,512]{1,0:T(8,128)}, f32[832,512]{1,0:T(8,128)}, f32[208,512]{1,0:T(8,128)}, f32[624,512]{1,0:T(8,128)}, bf16[416,512]{1,0:T(8,128)(2,1...) custom-call(bf16[1024,1664]{1,0:T(8,128)(2,1)} %get-tuple-element.78, ...), custom_call_target="tpu_custom_call" | custom-call | flops 20000000000 | bytes 100000000 | tf_op jit(solution)/shard_map/pallas_call | solution.py:1727
  385.6 16.7 %shard_map.460 = (bf16[400,512]{1,0:T(8,128)(2,1)}, f32[400,512]{1,0:T(8,128)}, f32[3,200,400]{2,1,0:T(8,128)}, f32[3,200,400]{2,1,0:T(8,128)}, f32[3,200,400]{2...) custom-call(f32[800,512]{1,0:T(8,128)} %get-tuple-element.97.refs_0_, ...), custom_call_target="tpu_custom_call" | custom-call | flops 20000000 | bytes 30000000 | tf_op jit(solution)/shard_map/pallas_call | solution.py:1850
